TPU v7x, 32 devices: a whole 2x2x4 slice. The times are simulated.
32 devices in a mesh: mp: 4 (over y, x), hidden: 8 (over z, core).
Axes of the slice: x: 2, y: 2, z: 4, core: 2. Of those that a mesh axis runs over, the one named last changes fastest.
Arguments:
- inputs: float32 [64, 8192], P('hidden', 'mp'), may hold values from -6 to 6
- weight: float32 [8192, 32768], P('mp', 'hidden'), may hold values from -0.0625 to 0.0625
- upstream: float32 [64, 32768], P('mp', 'hidden'), may hold values from -6 to 6
Outputs:
- input_grad: float32 [64, 8192], P('hidden', 'mp')
- weight_grad: float32 [8192, 32768], P('mp', 'hidden')
All inputs are finite; a program needn't handle non-finite values.
Results may differ from a plain program's by a relative error of at most 0.000092.
Values sent between devices are 32-bit elements; how exact they have to be, the bound alone decides.
No kernel may reach another device: no remote copies, remote signals or barrier semaphores. Data moves between devices by JAX's collectives and lax.ppermute only.
A program may use at most 192 MiB of HBM per device.

v0:
```python
import jax
import jax.numpy as jnp
from jax import lax
from jax.sharding import PartitionSpec as P


def gelu_slope(pre):
    cdf = 0.5 * (1.0 + jax.scipy.special.erf(pre * 0.7071067811865476))
    return cdf + pre * jnp.exp(-0.5 * pre * pre) * 0.3989422804014327


def body(inputs, weight, upstream):
    all_rows = lax.all_gather(inputs, "hidden", axis=0, tiled=True)
    block = all_rows
    pre_mine = lax.psum_scatter(
        jnp.dot(block, weight, preferred_element_type=jnp.float32, precision=lax.Precision.HIGHEST),
        "mp",
        scatter_dimension=0,
        tiled=True,
    )
    grad_mine = upstream * gelu_slope(pre_mine)
    grad_full = lax.all_gather(grad_mine, "mp", axis=0, tiled=True)
    weight_grad = lax.dot_general(
        all_rows,
        grad_full,
        (((0,), (0,)), ((), ())),
        precision=lax.Precision.HIGHEST,
        preferred_element_type=jnp.float32,
    )
    block = grad_full
    input_grad = lax.psum_scatter(
        lax.dot_general(
            block,
            weight,
            (((1,), (1,)), ((), ())),
            precision=lax.Precision.HIGHEST,
            preferred_element_type=jnp.float32,
        ),
        "hidden",
        scatter_dimension=0,
        tiled=True,
    )
    return (input_grad, weight_grad)


def solution(mesh):
    placed = (P("hidden", "mp"), P("mp", "hidden"), P("mp", "hidden"))
    return jax.shard_map(
        body,
        mesh=mesh,
        in_specs=placed,
        out_specs=(P("hidden", "mp"), P("mp", "hidden")),
        check_vma=False,
    )
```

profile of v0, /device:TPU:0, one launch (start us, length us, event | category | flops | bytes accessed | tf_op | source)
XLA Modules:
  0.0 214.1 jit_solution(12168822033753440640)
XLA Ops:
  7.2 0.0 copy-start.1
  7.2 0.0 reduce-scatter.3.cloned.1.call-start
  7.2 16.9 %all_gather.6 = f32[64,2048]{1,0:T(8,128)S(1)} all-gather(f32[8,2048]{1,0:T(8,128)} %param.3), channel_id=1, replica_groups=mesh['mp'=4,'hidden'=8] {'hidden'}, dimensions={0}, use_global_device_ids=true | all-gather | bytes 589824 | tf_op jit(solution)/shard_map/all_gather | solution.py:13
  24.1 25.0 %fusion.5 = f32[64,4096]{1,0:T(8,128)} fusion(f32[64,2048]{1,0:T(8,128)S(1)} %all_gather.6, f32[2048,4096]{1,0:T(8,128)} %param.4), kind=kOutput, calls=%fused_computation.7 | convolution fusion | flops 6442450944 | bytes 35127296 | tf_op jit(solution)/shard_map/dot_general | solution.py:16
  49.1 0.0 reduce-scatter.3.cloned.1.call-update
  49.2 0.0 all-gather.2.cloned.1.call-start
  49.2 28.9 %reduce-scatter.3.cloned.1.call-done = f32[16,4096]{1,0:T(8,128)} async-done(((f32[64,4096]{1,0:T(8,128)}), f32[16,4096]{1,0:T(8,128)}) %reduce-scatter.3.cloned.1.call-update) | async-done | bytes 262160 | tf_op jit(solution)/shard_map/reduce_scatter | solution.py:15
  78.1 0.0 copy-done.1
  78.1 1.8 fusion.4
  79.8 0.0 all-gather.2.cloned.1.call-update
  79.9 0.0 reduce-scatter.5.cloned.1.call-start
  79.9 27.4 %all-gather.2.cloned.1.call-done = f32[64,4096]{1,0:T(8,128)} async-done(((f32[16,4096]{1,0:T(8,128)}), f32[64,4096]{1,0:T(8,128)}) %all-gather.2.cloned.1.call-update) | async-done | bytes 1048592 | tf_op jit(solution)/shard_map/all_gather | solution.py:22
  107.3 0.0 copy-start
  107.3 38.8 %fusion.6 = f32[64,2048]{1,0:T(8,128)} fusion(f32[64,4096]{1,0:T(8,128)} %all-gather.2.cloned.1.call-done, f32[2048,4096]{1,0:T(8,128)} %param.4), kind=kOutput, calls=%fused_computation.8 | convolution fusion | flops 6442450944 | bytes 35127296 | tf_op jit(solution)/shard_map/dot_general | solution.py:32
  146.1 0.0 reduce-scatter.5.cloned.1.call-update
  146.2 0.0 copy-done
  146.2 30.3 %convolution_bitcast_fusion = f32[2048,4096]{0,1:T(8,128)} fusion(f32[64,4096]{1,0:T(8,128)S(1)} %copy-done, f32[64,2048]{1,0:T(8,128)S(1)} %all_gather.6), kind=kOutput, calls=%fused_computation | convolution fusion | flops 6442450944 | bytes 35127296 | tf_op jit(solution)/shard_map/dot_general | solution.py:23
  176.5 31.1 %copy.5 = f32[2048,4096]{1,0:T(8,128)} copy(f32[2048,4096]{0,1:T(8,128)} %convolution_bitcast_fusion) | data formatting | bytes 67108864
  207.6 0.0 reduce-scatter.5.cloned.1.call-done
Async XLA Ops:
  7.2 70.9 %copy-start.1 = (f32[16,4096]{1,0:T(8,128)S(1)}, f32[16,4096]{1,0:T(8,128)}, u32[]{:S(2)}) copy-start(f32[16,4096]{1,0:T(8,128)} %param.5) | copy-start | bytes 786436
  7.2 70.9 %reduce-scatter.3.cloned.1.call-start = ((), (), s32[]{:S(2)}) async-start(), calls=%async_computation.2 | async-start | bytes 1310720 | tf_op jit(solution)/shard_map/reduce_scatter | solution.py:15
  49.2 58.1 %all-gather.2.cloned.1.call-start = ((), (), s32[]{:S(2)}) async-start(), calls=%async_computation.3 | async-start | bytes 1310720 | tf_op jit(solution)/shard_map/all_gather | solution.py:22
  79.9 127.7 %reduce-scatter.5.cloned.1.call-start = ((), (), s32[]{:S(2)}) async-start(), calls=%async_computation.4 | async-start | bytes 589824 | tf_op jit(solution)/shard_map/reduce_scatter | solution.py:31
  107.3 38.9 %copy-start = (f32[64,4096]{1,0:T(8,128)S(1)}, f32[64,4096]{1,0:T(8,128)}, u32[]{:S(2)}) copy-start(f32[64,4096]{1,0:T(8,128)} %all-gather.2.cloned.1.call-done) | copy-start | bytes 3145732
Sparse Core Ops, SparseCore 0:
  49.3 28.7 reduce-scatter.2
  80.6 26.6 all-gather.1
  146.3 30.9 reduce-scatter.4
where the time goes:
time: 215 us; the launch traced here: 214 us
  matrix products  94.1 us (44%)
  waiting for transfers between devices  56.3 us (26%)
  local copies, waits for them, and re-layouts  31.1 us (14%)
  blocking collectives  16.9 us (8%)
  between operations  13.8 us (6%)
    dot_general x1, matrix products, body(): lax.dot_general(block, weight, (((1,), (1,)), ((), ())), precision=lax.Pr...  38.8 us
    unnamed x5, local copies, waits for them, and re-layouts  31.1 us
    dot_general x1, matrix products, body(): lax.dot_general(all_rows, grad_full, (((0,), (0,)), ((), ())), precision=...  30.3 us
    reduce_scatter x1, waiting for transfers between devices, body(): lax.psum_scatter(jnp.dot(block, weight, preferred_element_type=jnp.float3...  28.9 us
    all_gather x1, waiting for transfers between devices, body(): grad_full = lax.all_gather(grad_mine, 'mp', axis=0, tiled=True)  27.4 us
    dot_general x1, matrix products, body(): jnp.dot(block, weight, preferred_element_type=jnp.float32, precision=lax....  25 us
    all_gather x1, blocking collectives, body(): all_rows = lax.all_gather(inputs, 'hidden', axis=0, tiled=True)  16.9 us
  transfers between devices with their start and end apart: 3, of which 2 were waited for; matrix products, arithmetic and copies ran while one was open for 29% of the time, Pallas kernels for 0%

commit v1 on v0

v1 whole, which is shorter than its diff:
```python
import functools

import jax
import jax.numpy as jnp
from jax import lax
from jax.experimental import pallas as pl
from jax.experimental.pallas import tpu as pltpu
from jax.sharding import PartitionSpec as P

F32, BF16 = jnp.float32, jnp.bfloat16
MIB = 1 << 20
VMEM = pl.BlockSpec(memory_space=pltpu.VMEM)
CHUNKS = 2


def params(mib=12):
    return pltpu.CompilerParams(vmem_limit_bytes=mib * MIB)


def cost(flops, moved):
    return pl.CostEstimate(flops=int(flops), bytes_accessed=int(moved), transcendentals=0)


def fit(size, block):
    while size % block:
        block //= 2
    return block


def halves(value):
    high = value.astype(BF16)
    return high, (value - high.astype(F32)).astype(BF16)


def swap(value, axis, mask):
    size = lax.axis_size(axis)
    return lax.ppermute(value, axis, [(i, i ^ mask) for i in range(size)])


def split_kernel(rows, w_ref, high_ref, low_ref):
    at = pl.ds(pl.multiple_of(pl.program_id(0) * rows, rows), rows)
    high, low = halves(w_ref[...])
    high_ref[at, :] = high
    low_ref[at, :] = low


def split_weight(weight):
    deep, wide = weight.shape
    rows = fit(deep, 128)
    return pl.pallas_call(
        functools.partial(split_kernel, rows),
        grid=(deep // rows,),
        in_specs=[pl.BlockSpec((rows, wide), lambda i: (i, 0))],
        out_specs=[VMEM, VMEM],
        out_shape=[pltpu.VMEM((deep, wide), BF16)] * 2,
        compiler_params=params(),
        cost_estimate=cost(0, 8 * deep * wide),
        name="split_weight",
    )(weight)


def rows_kernel(n_mp, n_pair, *refs):
    pieces, (x_ref, flat) = refs[:n_pair], refs[n_pair:]
    pair = pieces[0].shape[0]
    z = lax.axis_index("hidden") // 2
    me = lax.axis_index("mp")
    for mask in range(n_pair):
        flat[pl.ds(pl.multiple_of((z ^ mask) * pair, pair), pair), :] = pieces[mask][...]
    rows = flat.shape[0]
    group = rows // n_mp
    for mask in range(n_mp):
        block = flat[pl.ds(pl.multiple_of((me ^ mask) * group, group), group), :]
        high, low = halves(block)
        x_ref[mask * group : (mask + 1) * group, :] = high
        x_ref[rows + mask * group : rows + (mask + 1) * group, :] = low


def order_rows(pieces, n_mp):
    pair, deep = pieces[0].shape
    rows = pair * len(pieces)
    return pl.pallas_call(
        functools.partial(rows_kernel, n_mp, len(pieces)),
        in_specs=[VMEM] * len(pieces),
        out_specs=VMEM,
        out_shape=jax.ShapeDtypeStruct((2 * rows, deep), BF16),
        scratch_shapes=[pltpu.VMEM((rows, deep), F32)],
        compiler_params=params(),
        cost_estimate=cost(0, 8 * rows * deep),
        name="order_rows",
    )(*pieces)


def turn_kernel(x_ref, t_ref):
    rows = x_ref.shape[0] // 2
    high = x_ref[:rows, :].astype(F32)
    low = x_ref[rows:, :].astype(F32)
    t_ref[...] = jnp.concatenate([high, high, low, low], axis=0).T.astype(BF16)


def turn_rows(x):
    two, deep = x.shape
    return pl.pallas_call(
        turn_kernel,
        in_specs=[VMEM],
        out_specs=VMEM,
        out_shape=jax.ShapeDtypeStruct((deep, 2 * two), BF16),
        compiler_params=params(),
        cost_estimate=cost(0, 4 * two * deep),
        name="turn_rows",
    )(x)


def pre_kernel(n_mp, first, block, x_ref, high_ref, low_ref, *outs):
    rows = x_ref.shape[0] // 2
    group = rows // n_mp

    def step(j, _):
        here = pl.ds(pl.multiple_of(j * block, block), block)
        there = pl.ds(pl.multiple_of(first + j * block, block), block)
        both = jnp.dot(x_ref[...], high_ref[:, there], preferred_element_type=F32)
        last = jnp.dot(x_ref[:rows, :], low_ref[:, there], preferred_element_type=F32)
        total = both[:rows] + both[rows:] + last
        for mask in range(n_mp):
            outs[mask][:, here] = total[mask * group : (mask + 1) * group]
        return 0

    lax.fori_loop(0, outs[0].shape[1] // block, step, 0)


def partial_pre(x, high, low, n_mp, first, count):
    rows, deep = x.shape[0] // 2, x.shape[1]
    return pl.pallas_call(
        functools.partial(pre_kernel, n_mp, first, fit(count, 512)),
        in_specs=[VMEM] * 3,
        out_specs=[VMEM] * n_mp,
        out_shape=[jax.ShapeDtypeStruct((rows // n_mp, count), F32)] * n_mp,
        compiler_params=params(),
        cost_estimate=cost(20 * rows * deep * count, 4 * rows * count),
        name="partial_pre",
    )(x, high, low)


def slope_kernel(first, *refs):
    parts, up_ref, out_ref = refs[:-2], refs[-2], refs[-1]
    pre = parts[0][...]
    for part in parts[1:]:
        pre = pre + part[...]
    cdf = 0.5 * (1.0 + lax.erf(pre * 0.7071067811865476))
    slope = cdf + pre * jnp.exp(-0.5 * pre * pre) * 0.3989422804014327
    out_ref[...] = up_ref[:, first : first + pre.shape[1]] * slope


def grad_mine(parts, upstream, first):
    rows, count = parts[0].shape
    return pl.pallas_call(
        functools.partial(slope_kernel, first),
        in_specs=[VMEM] * (len(parts) + 1),
        out_specs=VMEM,
        out_shape=jax.ShapeDtypeStruct((rows, count), F32),
        compiler_params=params(),
        cost_estimate=cost(0, 24 * rows * count),
        name="grad_mine",
    )(*parts, upstream)


def input_kernel(n_mp, first, block, has_total, is_last, high_ref, low_ref, *refs):
    pieces, refs = refs[:n_mp], refs[n_mp:]
    if has_total:
        total_ref, refs = refs[0], refs[1:]
    outs, (stack,) = refs[:-1], refs[-1:]
    group, count = pieces[0].shape
    rows = group * n_mp
    for mask in range(n_mp):
        at = slice(mask * group, (mask + 1) * group)
        high, low = halves(pieces[mask][...])
        stack[:, at] = high.astype(F32).T.astype(BF16)
        stack[:, rows + mask * group : rows + (mask + 1) * group] = low.astype(F32).T.astype(BF16)
    cols = slice(first, first + count)
    me = lax.axis_index("mp")
    hid = lax.axis_index("hidden")
    if is_last:
        keep_ref, send_ref, flat = outs
    else:
        (flat,) = outs

    def step(j, _):
        here = pl.ds(pl.multiple_of(j * block, block), block)
        both = jnp.dot(high_ref[here, cols], stack[...], preferred_element_type=F32)
        last = jnp.dot(low_ref[here, cols], stack[:, :rows], preferred_element_type=F32)
        total = (both[:, :rows] + both[:, rows:] + last).T
        if has_total:
            total = total + total_ref[:, here]
        if not is_last:
            flat[:, here] = total
            return 0
        for mask in range(n_mp):
            place = pl.ds(pl.multiple_of((me ^ mask) * group, group), group)
            flat[place, :] = total[mask * group : (mask + 1) * group]
        n_pair, size = keep_ref.shape[0], keep_ref.shape[1]
        for mask in range(n_pair):
            own = hid ^ (2 * mask)
            keep_ref[mask, :, here] = flat[pl.ds(pl.multiple_of(own * size, size), size), :]
            other = own ^ 1
            send_ref[mask, :, here] = flat[pl.ds(pl.multiple_of(other * size, size), size), :]
        return 0

    lax.fori_loop(0, high_ref.shape[0] // block, step, 0)


def input_share(high, low, pieces, total, first, n_hid, is_last):
    n_mp = len(pieces)
    group, count = pieces[0].shape
    rows, deep = group * n_mp, high.shape[0]
    block = fit(deep, 512)
    has_total = total is not None
    ins = [high, low, *pieces] + ([total] if has_total else [])
    scratch = [pltpu.VMEM((count, 2 * rows), BF16)]
    if is_last:
        one = jax.ShapeDtypeStruct((n_hid // 2, rows // n_hid, deep), F32)
        shapes = [one, one]
        scratch = [pltpu.VMEM((rows, block), F32)] + scratch
    else:
        shapes = [jax.ShapeDtypeStruct((rows, deep), F32)]
    return pl.pallas_call(
        functools.partial(input_kernel, n_mp, first, block, has_total, is_last),
        in_specs=[VMEM] * len(ins),
        out_specs=[VMEM] * len(shapes),
        out_shape=shapes,
        scratch_shapes=scratch,
        compiler_params=params(),
        cost_estimate=cost(30 * rows * deep * count, 8 * rows * deep),
        name="input_share",
    )(*ins)


def pair_kernel(*refs):
    keep_ref, got_ref, outs = refs[0], refs[1], refs[2:]
    for mask in range(len(outs)):
        outs[mask][...] = keep_ref[mask] + got_ref[mask]


def pair_sums(keep, got):
    n, size, deep = keep.shape
    return pl.pallas_call(
        pair_kernel,
        in_specs=[VMEM] * 2,
        out_specs=[VMEM] * n,
        out_shape=[jax.ShapeDtypeStruct((size, deep), F32)] * n,
        compiler_params=params(),
        cost_estimate=cost(0, 12 * n * size * deep),
        name="pair_sums",
    )(keep, got)


def add_kernel(*refs):
    total = refs[0][...]
    for ref in refs[1:-1]:
        total = total + ref[...]
    refs[-1][...] = total


def add_up(parts):
    return pl.pallas_call(
        add_kernel,
        in_specs=[VMEM] * len(parts),
        out_specs=VMEM,
        out_shape=jax.ShapeDtypeStruct(parts[0].shape, F32),
        compiler_params=params(),
        name="add_up",
    )(*parts)


def weight_kernel(n_mp, has_base, t_ref, *refs):
    pieces, out_ref, stack = refs[:n_mp], refs[-2], refs[-1]
    group = pieces[0].shape[0]
    rows = group * n_mp

    @pl.when(pl.program_id(0) == 0)
    def _():
        for mask in range(n_mp):
            high, low = halves(pieces[mask][...])
            for copy, part in enumerate((high, low, high, low)):
                at = copy * rows + mask * group
                stack[at : at + group, :] = part

    out_ref[...] = jnp.dot(t_ref[...], stack[...], preferred_element_type=F32)


def weight_part(turned, pieces, base, index, wide):
    n_mp = len(pieces)
    group, count = pieces[0].shape
    rows, deep = group * n_mp, turned.shape[0]
    block = fit(deep, 256)
    has_base = base is not None
    ins = [turned, *pieces] + ([base] if has_base else [])
    specs = [pl.BlockSpec((block, 4 * rows), lambda i: (i, 0))] + [VMEM] * n_mp
    if has_base:
        specs.append(pl.BlockSpec(memory_space=pl.ANY))
    return pl.pallas_call(
        functools.partial(weight_kernel, n_mp, has_base),
        grid=(deep // block,),
        in_specs=specs,
        out_specs=pl.BlockSpec((block, count), lambda i: (i, index)),
        out_shape=jax.ShapeDtypeStruct((deep, wide), F32),
        scratch_shapes=[pltpu.VMEM((4 * rows, count), BF16)],
        input_output_aliases={len(ins) - 1: 0} if has_base else {},
        compiler_params=params(14),
        cost_estimate=cost(0, 4 * deep * count),
        name="weight_part",
    )(*ins)


def body(inputs, weight, upstream):
    n_mp, n_hid = lax.axis_size("mp"), lax.axis_size("hidden")
    wide = weight.shape[1]
    count = wide // CHUNKS
    starts = [c * count for c in range(CHUNKS)]

    partner = swap(inputs, "hidden", 1)
    even = lax.axis_index("hidden") % 2 == 0
    pair = jnp.concatenate([jnp.where(even, inputs, partner), jnp.where(even, partner, inputs)], axis=0)
    pieces = [pair] + [swap(pair, "hidden", 2 * mask) for mask in range(1, n_hid // 2)]
    high, low = split_weight(weight)
    x = order_rows(pieces, n_mp)
    turned = turn_rows(x)

    parts = [partial_pre(x, high, low, n_mp, first, count) for first in starts]
    mine = []
    for first, own in zip(starts, parts):
        got = [own[0]] + [swap(own[mask], "mp", mask) for mask in range(1, n_mp)]
        mine.append(grad_mine(got, upstream, first))
    grads = [[own] + [swap(own, "mp", mask) for mask in range(1, n_mp)] for own in mine]

    total, weight_grad = None, None
    for c, first in enumerate(starts):
        is_last = c == CHUNKS - 1
        out = input_share(high, low, grads[c], total, first, n_hid, is_last)
        if not is_last:
            total = out[0]
        weight_grad = weight_part(turned, grads[c], weight_grad, c, wide)
    keep, send = out
    sums = pair_sums(keep, swap(send, "hidden", 1))
    input_grad = add_up([sums[0]] + [swap(sums[mask], "hidden", 2 * mask) for mask in range(1, n_hid // 2)])
    return input_grad, weight_grad


def solution(mesh):
    placed = (P("hidden", "mp"), P("mp", "hidden"), P("mp", "hidden"))
    return jax.shard_map(
        body,
        mesh=mesh,
        in_specs=placed,
        out_specs=(P("hidden", "mp"), P("mp", "hidden")),
        check_vma=False,
    )
```

time: 215 us -> 93.6 us (0.44)
  matrix products: 94.1 us -> 0 us
  Pallas kernels: 0 us -> 57.8 us
  waiting for transfers between devices: 56.3 us -> 7.71 us
  local copies, waits for them, and re-layouts: 31.1 us -> 0.01 us
  starting transfers between devices: 0.12 us -> 26.2 us
  blocking collectives: 16.9 us -> 0 us
  between operations: 13.8 us -> 0.78 us
    dot_general x3 -> x0, matrix products: 94.1 us -> none  [the longest x1 38.8 us: body(): lax.dot_general(block, weight, (((1,), (1,)), ((), ())), precision=lax.Pr...]
    pallas_call x0 -> x13, Pallas kernels: none -> 57.8 us  [the longest x2 17.7 us: input_share(): pl.pallas_call(functools.partial(input_kernel, n_mp, first, block, has_to...]
    unnamed x5 -> x2, local copies, waits for them, and re-layouts: 31.1 us -> 0.01 us
    reduce_scatter x2 -> x0, waiting for transfers between devices: 28.9 us -> none  [the longest x1 28.9 us: body(): lax.psum_scatter(jnp.dot(block, weight, preferred_element_type=jnp.float3...]
    all_gather x1 -> x0, waiting for transfers between devices: 27.4 us -> none  [body(): grad_full = lax.all_gather(grad_mine, 'mp', axis=0, tiled=True)]
    ppermute x0 -> x20, starting transfers between devices: none -> 26.2 us  [swap(): return lax.ppermute(value, axis, [(i, i ^ mask) for i in range(size)])]
    all_gather x1 -> x0, blocking collectives: 16.9 us -> none  [body(): all_rows = lax.all_gather(inputs, 'hidden', axis=0, tiled=True)]
    ppermute x0 -> x20, waiting for transfers between devices: none -> 7.71 us  [swap(): return lax.ppermute(value, axis, [(i, i ^ mask) for i in range(size)])]
  transfers between devices with their start and end apart: 3 -> 20, of which waited for: 2 -> 3; matrix products, arithmetic and copies ran while one was open for 29% -> 0% of each run, Pallas kernels for 0% -> 48%
where the time goes in v1:
time: 93.6 us; the launch traced here: 93.4 us
  Pallas kernels  57.8 us (62%)
  starting transfers between devices  26.2 us (28%)
  waiting for transfers between devices  7.71 us (8%)
    ppermute x20, starting transfers between devices, swap(): return lax.ppermute(value, axis, [(i, i ^ mask) for i in range(size)])  26.2 us
    pallas_call x2, Pallas kernels, input_share(): pl.pallas_call(functools.partial(input_kernel, n_mp, first, block, has_to...  17.7 us
    pallas_call x1, Pallas kernels, split_weight(): pl.pallas_call(functools.partial(split_kernel, rows), grid=(deep // rows,...  16.9 us
    pallas_call x2, Pallas kernels, weight_part(): pl.pallas_call(functools.partial(weight_kernel, n_mp, has_base), grid=(de...  15.6 us
    ppermute x20, waiting for transfers between devices, swap(): return lax.ppermute(value, axis, [(i, i ^ mask) for i in range(size)])  7.71 us
    pallas_call x2, Pallas kernels, partial_pre(): pl.pallas_call(functools.partial(pre_kernel, n_mp, first, fit(count, 512)...  6.27 us
  transfers between devices with their start and end apart: 20, of which 3 were waited for; matrix products, arithmetic and copies ran while one was open for 0% of the time, Pallas kernels for 48%

profile of v1, /device:TPU:0, one launch (start us, length us, event | category | flops | bytes accessed | tf_op | source)
XLA Modules:
  0.0 93.4 jit_solution(17837290183845648493)
XLA Ops:
  0.6 0.5 collective-permute-start
  1.1 1.1 %collective-permute-done = f32[8,2048]{1,0:T(8,128)S(1)} collective-permute-done((f32[8,2048]{1,0:T(8,128)}, f32[8,2048]{1,0:T(8,128)S(1)}, u32[]{:S(2)}, u32[]{:S(2)}) %collective-permute-start) | collective-permute-done | bytes 65568 | tf_op jit(solution)/shard_map/ppermute | solution.py:37
  2.3 0.8 broadcast_select_fusion.1
  3.1 5.0 %collective-permute-start.3 = (f32[16,2048]{1,0:T(8,128)S(1)}, f32[16,2048]{1,0:T(8,128)S(1)}, u32[]{:S(2)}, u32[]{:S(2)}) collective-permute-start(f32[16,2048]{1,0:T(8,128)S(1)} %pad_maximum_fusion.refs_0_), channel_id=1, source_target_pairs={{0,6},{1,7},{2,4},{3,5},{4,2},{5,3},{6,0},{7,1},{8,14},{9,15},{10,... | collective-permute-start | bytes 393224 | tf_op jit(solution)/shard_map/ppermute | solution.py:37
  8.2 0.6 collective-permute-start.1
  8.8 16.9 %split_weight.1 = (bf16[2048,4096]{1,0:T(8,128)(2,1)S(1)}, bf16[2048,4096]{1,0:T(8,128)(2,1)S(1)}) custom-call(f32[2048,4096]{1,0:T(8,128)} %w_ref.1), custom_call_target="tpu_custom_call" | custom-call | bytes 67108864 | tf_op jit(solution)/shard_map/split_weight/pallas_call | solution.py:50
  25.7 0.1 order_rows.1.x_ref
  25.9 3.1 %partial_pre.3 = (f32[16,2048]{1,0:T(8,128)S(1)}, f32[16,2048]{1,0:T(8,128)S(1)}, f32[16,2048]{1,0:T(8,128)S(1)}, f32[16,2048]{1,0:T(8,128)S(1)}) custom-call(bf16[128,2048]{1,0:T(8,128)(2,1)S(1)} %order_rows.1.x_ref, bf16[2048,4096]{1,0:T(8,128)(2,1)S(1)} %get-tuple-element.18.high_ref, bf16[2048,4096]{1,0:T(8,128)(2,1)S(1)} %get-tuple-element.19.low_ref), custom_call_target="tpu_custom_call" | custom-call | flops 5368709120 | bytes 524288 | tf_op jit(solution)/shard_map/partial_pre/pallas_call | solution.py:132
  29.0 1.7 %collective-permute-start.10 = (f32[16,2048]{1,0:T(8,128)S(1)}, f32[16,2048]{1,0:T(8,128)S(1)}, u32[]{:S(2)}, u32[]{:S(2)}) collective-permute-start(f32[16,2048]{1,0:T(8,128)S(1)} %get-tuple-element.25), channel_id=1, source_target_pairs={{0,8},{8,0},{16,24},{24,16},{1,9},{9,1},{17,25},{25,17},{2,10},{10... | collective-permute-start | bytes 393224 | tf_op jit(solution)/shard_map/ppermute | solution.py:37
  30.7 1.5 %collective-permute-start.11 = (f32[16,2048]{1,0:T(8,128)S(1)}, f32[16,2048]{1,0:T(8,128)S(1)}, u32[]{:S(2)}, u32[]{:S(2)}) collective-permute-start(f32[16,2048]{1,0:T(8,128)S(1)} %get-tuple-element.26), channel_id=1, source_target_pairs={{0,16},{8,24},{16,0},{24,8},{1,17},{9,25},{17,1},{25,9},{2,18},{10... | collective-permute-start | bytes 393224 | tf_op jit(solution)/shard_map/ppermute | solution.py:37
  32.2 0.3 collective-permute-start.12
  32.6 3.1 %partial_pre.2 = (f32[16,2048]{1,0:T(8,128)S(1)}, f32[16,2048]{1,0:T(8,128)S(1)}, f32[16,2048]{1,0:T(8,128)S(1)}, f32[16,2048]{1,0:T(8,128)S(1)}) custom-call(bf16[128,2048]{1,0:T(8,128)(2,1)S(1)} %order_rows.1.x_ref, bf16[2048,4096]{1,0:T(8,128)(2,1)S(1)} %get-tuple-element.18.high_ref, bf16[2048,4096]{1,0:T(8,128)(2,1)S(1)} %get-tuple-element.19.low_ref), custom_call_target="tpu_custom_call" | custom-call | flops 5368709120 | bytes 524288 | tf_op jit(solution)/shard_map/partial_pre/pallas_call | solution.py:132
  35.7 1.7 %collective-permute-start.4 = (f32[16,2048]{1,0:T(8,128)S(1)}, f32[16,2048]{1,0:T(8,128)S(1)}, u32[]{:S(2)}, u32[]{:S(2)}) collective-permute-start(f32[16,2048]{1,0:T(8,128)S(1)} %get-tuple-element.21), channel_id=1, source_target_pairs={{0,8},{8,0},{16,24},{24,16},{1,9},{9,1},{17,25},{25,17},{2,10},{10... | collective-permute-start | bytes 393224 | tf_op jit(solution)/shard_map/ppermute | solution.py:37
  37.4 1.5 %collective-permute-start.5 = (f32[16,2048]{1,0:T(8,128)S(1)}, f32[16,2048]{1,0:T(8,128)S(1)}, u32[]{:S(2)}, u32[]{:S(2)}) collective-permute-start(f32[16,2048]{1,0:T(8,128)S(1)} %get-tuple-element.22), channel_id=1, source_target_pairs={{0,16},{8,24},{16,0},{24,8},{1,17},{9,25},{17,1},{25,9},{2,18},{10... | collective-permute-start | bytes 393224 | tf_op jit(solution)/shard_map/ppermute | solution.py:37
  38.9 0.3 collective-permute-start.6
  39.4 2.7 %collective-permute-start.15 = (f32[16,2048]{1,0:T(8,128)S(1)}, f32[16,2048]{1,0:T(8,128)S(1)}, u32[]{:S(2)}, u32[]{:S(2)}) collective-permute-start(f32[16,2048]{1,0:T(8,128)S(1)} %grad_mine.3.refs_0_), channel_id=1, source_target_pairs={{0,24},{8,16},{16,8},{24,0},{1,25},{9,17},{17,9},{25,1},{2,26},{10... | collective-permute-start | bytes 393224 | tf_op jit(solution)/shard_map/ppermute | solution.py:37
  42.0 0.5 collective-permute-start.14
  42.6 0.8 collective-permute-start.13
  43.3 5.0 %collective-permute-done.5.refs_2_ = f32[16,2048]{1,0:T(8,128)S(1)} collective-permute-done((f32[16,2048]{1,0:T(8,128)S(1)}, f32[16,2048]{1,0:T(8,128)S(1)}, u32[]{:S(2)}, u32[]{:S(2)}) %collective-permute-start.5) | collective-permute-done | bytes 131104 | tf_op jit(solution)/shard_map/ppermute | solution.py:37
  48.4 2.0 %collective-permute-start.9 = (f32[16,2048]{1,0:T(8,128)S(1)}, f32[16,2048]{1,0:T(8,128)S(1)}, u32[]{:S(2)}, u32[]{:S(2)}) collective-permute-start(f32[16,2048]{1,0:T(8,128)S(1)} %grad_mine.2.refs_0_), channel_id=1, source_target_pairs={{0,24},{8,16},{16,8},{24,0},{1,25},{9,17},{17,9},{25,1},{2,26},{10... | collective-permute-start | bytes 393224 | tf_op jit(solution)/shard_map/ppermute | solution.py:37
  50.4 1.1 %collective-permute-start.8 = (f32[16,2048]{1,0:T(8,128)S(1)}, f32[16,2048]{1,0:T(8,128)S(1)}, u32[]{:S(2)}, u32[]{:S(2)}) collective-permute-start(f32[16,2048]{1,0:T(8,128)S(1)} %grad_mine.2.refs_0_), channel_id=1, source_target_pairs={{0,16},{8,24},{16,0},{24,8},{1,17},{9,25},{17,1},{25,9},{2,18},{10... | collective-permute-start | bytes 393224 | tf_op jit(solution)/shard_map/ppermute | solution.py:37
  51.6 1.4 %collective-permute-start.7 = (f32[16,2048]{1,0:T(8,128)S(1)}, f32[16,2048]{1,0:T(8,128)S(1)}, u32[]{:S(2)}, u32[]{:S(2)}) collective-permute-start(f32[16,2048]{1,0:T(8,128)S(1)} %grad_mine.2.refs_0_), channel_id=1, source_target_pairs={{0,8},{8,0},{16,24},{24,16},{1,9},{9,1},{17,25},{25,17},{2,10},{10... | collective-permute-start | bytes 393224 | tf_op jit(solution)/shard_map/ppermute | solution.py:37
  52.9 8.8 %input_share.2.refs_4_ = f32[64,2048]{1,0:T(8,128)S(1)} custom-call(bf16[2048,4096]{1,0:T(8,128)(2,1)S(1)} %get-tuple-element.18.high_ref, bf16[2048,4096]{1,0:T(8,128)(2,1)S(1)} %get-tuple-element.19.low_ref, f32[16,2048]{1,0:T(8,128)S(1)} %grad_mine.3.refs_0_, f32[16,2048]{1,0:T(8,128)S(1)} %collective-permute-done.13.refs_1_, ...), custom_call_target="tpu_custom_call" | custom-call | flops 8053063680 | bytes 1048576 | tf_op jit(solution)/shard_map/input_share/pallas_call | solution.py:224
  61.8 8.9 %input_share.3 = (f32[4,8,2048]{2,1,0:T(8,128)S(1)}, f32[4,8,2048]{2,1,0:T(8,128)S(1)}) custom-call(bf16[2048,4096]{1,0:T(8,128)(2,1)S(1)} %get-tuple-element.18.high_ref, bf16[2048,4096]{1,0:T(8,128)(2,1)S(1)} %get-tuple-element.19.low_ref, f32[16,2048]{1,0:T(8,128)S(1)} %grad_mine.2.refs_0_, f32[16,2048]{1,0:T(8,128)S(1)} %collective-permute-done.7.refs_1_, ...), custom_call_target="tpu_custom_call" | custom-call | flops 8053063680 | bytes 1048576 | tf_op jit(solution)/shard_map/input_share/pallas_call | solution.py:224
  70.7 1.5 %collective-permute-done.16.refs_1_ = f32[4,8,2048]{2,1,0:T(8,128)S(1)} collective-permute-done((f32[4,8,2048]{2,1,0:T(8,128)S(1)}, f32[4,8,2048]{2,1,0:T(8,128)S(1)}, u32[]{:S(2)}, u32[]{:S(2)}) %collective-permute-start.16) | collective-permute-done | bytes 262176 | tf_op jit(solution)/shard_map/ppermute | solution.py:37
  72.3 1.2 %collective-permute-start.17 = (f32[8,2048]{1,0:T(8,128)S(1)}, f32[8,2048]{1,0:T(8,128)S(1)}, u32[]{:S(2)}, u32[]{:S(2)}) collective-permute-start(f32[8,2048]{1,0:T(8,128)S(1)} %get-tuple-element.31), channel_id=1, source_target_pairs={{0,2},{1,3},{2,0},{3,1},{4,6},{5,7},{6,4},{7,5},{8,10},{9,11},{10,... | collective-permute-start | bytes 196616 | tf_op jit(solution)/shard_map/ppermute | solution.py:37
  73.5 2.9 %collective-permute-start.18 = (f32[8,2048]{1,0:T(8,128)S(1)}, f32[8,2048]{1,0:T(8,128)S(1)}, u32[]{:S(2)}, u32[]{:S(2)}) collective-permute-start(f32[8,2048]{1,0:T(8,128)S(1)} %get-tuple-element.32), channel_id=1, source_target_pairs={{0,4},{1,5},{2,6},{3,7},{4,0},{5,1},{6,2},{7,3},{8,12},{9,13},{10,... | collective-permute-start | bytes 196616 | tf_op jit(solution)/shard_map/ppermute | solution.py:37
  76.4 0.4 collective-permute-start.19
  76.8 0.3 turn_rows.1.t_ref
  77.1 7.8 %weight_part.2.refs_4_ = f32[2048,4096]{1,0:T(8,128)} custom-call(bf16[2048,256]{1,0:T(8,128)(2,1)S(1)} %turn_rows.1.t_ref, f32[16,2048]{1,0:T(8,128)S(1)} %grad_mine.3.refs_0_, f32[16,2048]{1,0:T(8,128)S(1)} %collective-permute-done.13.refs_1_, f32[16,2048]{1,0:T(8,128)S(1)} %collective-permute-done.14.refs_2_, f32[16,2048]{1,0:T(8,128)S(1)} %collective-permute-done.15.refs_3_), custom_call_target="tpu_custom_call" | custom-call | bytes 16777216 | tf_op jit(solution)/shard_map/weight_part/pallas_call | solution.py:299
  84.9 7.8 %weight_part.3 = f32[2048,4096]{1,0:T(8,128)} custom-call(bf16[2048,256]{1,0:T(8,128)(2,1)S(1)} %turn_rows.1.t_ref, f32[16,2048]{1,0:T(8,128)S(1)} %grad_mine.2.refs_0_, f32[16,2048]{1,0:T(8,128)S(1)} %collective-permute-done.7.refs_1_, f32[16,2048]{1,0:T(8,128)S(1)} %collective-permute-done.8.refs_2_, ...), custom_call_target="tpu_custom_call", output_to_operand_aliasing={{}: (5, {})} | custom-call | bytes 16777216 | tf_op jit(solution)/shard_map/weight_part/pallas_call | solution.py:299
  92.7 0.6 add_up.1
  (25 shorter events, 0.3 us)
Async XLA Ops:
  0.6 1.6 %collective-permute-start = (f32[8,2048]{1,0:T(8,128)}, f32[8,2048]{1,0:T(8,128)S(1)}, u32[]{:S(2)}, u32[]{:S(2)}) collective-permute-start(f32[8,2048]{1,0:T(8,128)} %param.3), channel_id=1, source_target_pairs={{0,1},{1,0},{2,3},{3,2},{4,5},{5,4},{6,7},{7,6},{8,9},{9,8},{10,11... | collective-permute-start | bytes 196616 | tf_op jit(solution)/shard_map/ppermute | solution.py:37
  3.1 22.6 %collective-permute-start.3 = (f32[16,2048]{1,0:T(8,128)S(1)}, f32[16,2048]{1,0:T(8,128)S(1)}, u32[]{:S(2)}, u32[]{:S(2)}) collective-permute-start(f32[16,2048]{1,0:T(8,128)S(1)} %pad_maximum_fusion.refs_0_), channel_id=1, source_target_pairs={{0,6},{1,7},{2,4},{3,5},{4,2},{5,3},{6,0},{7,1},{8,14},{9,15},{10,... | collective-permute-start | bytes 393224 | tf_op jit(solution)/shard_map/ppermute | solution.py:37
  8.1 17.6 %collective-permute-start.2 = (f32[16,2048]{1,0:T(8,128)S(1)}, f32[16,2048]{1,0:T(8,128)S(1)}, u32[]{:S(2)}, u32[]{:S(2)}) collective-permute-start(f32[16,2048]{1,0:T(8,128)S(1)} %pad_maximum_fusion.refs_0_), channel_id=1, source_target_pairs={{0,4},{1,5},{2,6},{3,7},{4,0},{5,1},{6,2},{7,3},{8,12},{9,13},{10,... | collective-permute-start | bytes 393224 | tf_op jit(solution)/shard_map/ppermute | solution.py:37
  8.2 17.6 %collective-permute-start.1 = (f32[16,2048]{1,0:T(8,128)S(1)}, f32[16,2048]{1,0:T(8,128)S(1)}, u32[]{:S(2)}, u32[]{:S(2)}) collective-permute-start(f32[16,2048]{1,0:T(8,128)S(1)} %pad_maximum_fusion.refs_0_), channel_id=1, source_target_pairs={{0,2},{1,3},{2,0},{3,1},{4,6},{5,7},{6,4},{7,5},{8,10},{9,11},{10,... | collective-permute-start | bytes 393224 | tf_op jit(solution)/shard_map/ppermute | solution.py:37
  25.9 13.4 %copy-start = (f32[16,4096]{1,0:T(8,128)S(1)}, f32[16,4096]{1,0:T(8,128)}, u32[]{:S(2)}) copy-start(f32[16,4096]{1,0:T(8,128)} %refs_4_.3) | copy-start | bytes 786436
  29.0 9.9 %collective-permute-start.10 = (f32[16,2048]{1,0:T(8,128)S(1)}, f32[16,2048]{1,0:T(8,128)S(1)}, u32[]{:S(2)}, u32[]{:S(2)}) collective-permute-start(f32[16,2048]{1,0:T(8,128)S(1)} %get-tuple-element.25), channel_id=1, source_target_pairs={{0,8},{8,0},{16,24},{24,16},{1,9},{9,1},{17,25},{25,17},{2,10},{10... | collective-permute-start | bytes 393224 | tf_op jit(solution)/shard_map/ppermute | solution.py:37
  30.7 8.6 %collective-permute-start.11 = (f32[16,2048]{1,0:T(8,128)S(1)}, f32[16,2048]{1,0:T(8,128)S(1)}, u32[]{:S(2)}, u32[]{:S(2)}) collective-permute-start(f32[16,2048]{1,0:T(8,128)S(1)} %get-tuple-element.26), channel_id=1, source_target_pairs={{0,16},{8,24},{16,0},{24,8},{1,17},{9,25},{17,1},{25,9},{2,18},{10... | collective-permute-start | bytes 393224 | tf_op jit(solution)/shard_map/ppermute | solution.py:37
  32.2 7.0 %collective-permute-start.12 = (f32[16,2048]{1,0:T(8,128)S(1)}, f32[16,2048]{1,0:T(8,128)S(1)}, u32[]{:S(2)}, u32[]{:S(2)}) collective-permute-start(f32[16,2048]{1,0:T(8,128)S(1)} %get-tuple-element.27), channel_id=1, source_target_pairs={{0,24},{8,16},{16,8},{24,0},{1,25},{9,17},{17,9},{25,1},{2,26},{10... | collective-permute-start | bytes 393224 | tf_op jit(solution)/shard_map/ppermute | solution.py:37
  35.7 6.8 %collective-permute-start.4 = (f32[16,2048]{1,0:T(8,128)S(1)}, f32[16,2048]{1,0:T(8,128)S(1)}, u32[]{:S(2)}, u32[]{:S(2)}) collective-permute-start(f32[16,2048]{1,0:T(8,128)S(1)} %get-tuple-element.21), channel_id=1, source_target_pairs={{0,8},{8,0},{16,24},{24,16},{1,9},{9,1},{17,25},{25,17},{2,10},{10... | collective-permute-start | bytes 393224 | tf_op jit(solution)/shard_map/ppermute | solution.py:37
  37.4 10.9 %collective-permute-start.5 = (f32[16,2048]{1,0:T(8,128)S(1)}, f32[16,2048]{1,0:T(8,128)S(1)}, u32[]{:S(2)}, u32[]{:S(2)}) collective-permute-start(f32[16,2048]{1,0:T(8,128)S(1)} %get-tuple-element.22), channel_id=1, source_target_pairs={{0,16},{8,24},{16,0},{24,8},{1,17},{9,25},{17,1},{25,9},{2,18},{10... | collective-permute-start | bytes 393224 | tf_op jit(solution)/shard_map/ppermute | solution.py:37
  38.9 9.4 %collective-permute-start.6 = (f32[16,2048]{1,0:T(8,128)S(1)}, f32[16,2048]{1,0:T(8,128)S(1)}, u32[]{:S(2)}, u32[]{:S(2)}) collective-permute-start(f32[16,2048]{1,0:T(8,128)S(1)} %get-tuple-element.23), channel_id=1, source_target_pairs={{0,24},{8,16},{16,8},{24,0},{1,25},{9,17},{17,9},{25,1},{2,26},{10... | collective-permute-start | bytes 393224 | tf_op jit(solution)/shard_map/ppermute | solution.py:37
  39.4 12.2 %collective-permute-start.15 = (f32[16,2048]{1,0:T(8,128)S(1)}, f32[16,2048]{1,0:T(8,128)S(1)}, u32[]{:S(2)}, u32[]{:S(2)}) collective-permute-start(f32[16,2048]{1,0:T(8,128)S(1)} %grad_mine.3.refs_0_), channel_id=1, source_target_pairs={{0,24},{8,16},{16,8},{24,0},{1,25},{9,17},{17,9},{25,1},{2,26},{10... | collective-permute-start | bytes 393224 | tf_op jit(solution)/shard_map/ppermute | solution.py:37
  42.0 10.9 %collective-permute-start.14 = (f32[16,2048]{1,0:T(8,128)S(1)}, f32[16,2048]{1,0:T(8,128)S(1)}, u32[]{:S(2)}, u32[]{:S(2)}) collective-permute-start(f32[16,2048]{1,0:T(8,128)S(1)} %grad_mine.3.refs_0_), channel_id=1, source_target_pairs={{0,16},{8,24},{16,0},{24,8},{1,17},{9,25},{17,1},{25,9},{2,18},{10... | collective-permute-start | bytes 393224 | tf_op jit(solution)/shard_map/ppermute | solution.py:37
  42.6 10.4 %collective-permute-start.13 = (f32[16,2048]{1,0:T(8,128)S(1)}, f32[16,2048]{1,0:T(8,128)S(1)}, u32[]{:S(2)}, u32[]{:S(2)}) collective-permute-start(f32[16,2048]{1,0:T(8,128)S(1)} %grad_mine.3.refs_0_), channel_id=1, source_target_pairs={{0,8},{8,0},{16,24},{24,16},{1,9},{9,1},{17,25},{25,17},{2,10},{10... | collective-permute-start | bytes 393224 | tf_op jit(solution)/shard_map/ppermute | solution.py:37
  48.4 13.3 %collective-permute-start.9 = (f32[16,2048]{1,0:T(8,128)S(1)}, f32[16,2048]{1,0:T(8,128)S(1)}, u32[]{:S(2)}, u32[]{:S(2)}) collective-permute-start(f32[16,2048]{1,0:T(8,128)S(1)} %grad_mine.2.refs_0_), channel_id=1, source_target_pairs={{0,24},{8,16},{16,8},{24,0},{1,25},{9,17},{17,9},{25,1},{2,26},{10... | collective-permute-start | bytes 393224 | tf_op jit(solution)/shard_map/ppermute | solution.py:37
  50.4 11.3 %collective-permute-start.8 = (f32[16,2048]{1,0:T(8,128)S(1)}, f32[16,2048]{1,0:T(8,128)S(1)}, u32[]{:S(2)}, u32[]{:S(2)}) collective-permute-start(f32[16,2048]{1,0:T(8,128)S(1)} %grad_mine.2.refs_0_), channel_id=1, source_target_pairs={{0,16},{8,24},{16,0},{24,8},{1,17},{9,25},{17,1},{25,9},{2,18},{10... | collective-permute-start | bytes 393224 | tf_op jit(solution)/shard_map/ppermute | solution.py:37
  51.6 10.2 %collective-permute-start.7 = (f32[16,2048]{1,0:T(8,128)S(1)}, f32[16,2048]{1,0:T(8,128)S(1)}, u32[]{:S(2)}, u32[]{:S(2)}) collective-permute-start(f32[16,2048]{1,0:T(8,128)S(1)} %grad_mine.2.refs_0_), channel_id=1, source_target_pairs={{0,8},{8,0},{16,24},{24,16},{1,9},{9,1},{17,25},{25,17},{2,10},{10... | collective-permute-start | bytes 393224 | tf_op jit(solution)/shard_map/ppermute | solution.py:37
  70.7 1.6 %collective-permute-start.16 = (f32[4,8,2048]{2,1,0:T(8,128)S(1)}, f32[4,8,2048]{2,1,0:T(8,128)S(1)}, u32[]{:S(2)}, u32[]{:S(2)}) collective-permute-start(f32[4,8,2048]{2,1,0:T(8,128)S(1)} %get-tuple-element.29), channel_id=1, source_target_pairs={{0,1},{1,0},{2,3},{3,2},{4,5},{5,4},{6,7},{7,6},{8,9},{9,8},{10,11... | collective-permute-start | bytes 786440 | tf_op jit(solution)/shard_map/ppermute | solution.py:37
  72.3 20.4 %collective-permute-start.17 = (f32[8,2048]{1,0:T(8,128)S(1)}, f32[8,2048]{1,0:T(8,128)S(1)}, u32[]{:S(2)}, u32[]{:S(2)}) collective-permute-start(f32[8,2048]{1,0:T(8,128)S(1)} %get-tuple-element.31), channel_id=1, source_target_pairs={{0,2},{1,3},{2,0},{3,1},{4,6},{5,7},{6,4},{7,5},{8,10},{9,11},{10,... | collective-permute-start | bytes 196616 | tf_op jit(solution)/shard_map/ppermute | solution.py:37
  73.5 19.2 %collective-permute-start.18 = (f32[8,2048]{1,0:T(8,128)S(1)}, f32[8,2048]{1,0:T(8,128)S(1)}, u32[]{:S(2)}, u32[]{:S(2)}) collective-permute-start(f32[8,2048]{1,0:T(8,128)S(1)} %get-tuple-element.32), channel_id=1, source_target_pairs={{0,4},{1,5},{2,6},{3,7},{4,0},{5,1},{6,2},{7,3},{8,12},{9,13},{10,... | collective-permute-start | bytes 196616 | tf_op jit(solution)/shard_map/ppermute | solution.py:37
  76.4 16.4 %collective-permute-start.19 = (f32[8,2048]{1,0:T(8,128)S(1)}, f32[8,2048]{1,0:T(8,128)S(1)}, u32[]{:S(2)}, u32[]{:S(2)}) collective-permute-start(f32[8,2048]{1,0:T(8,128)S(1)} %get-tuple-element.33), channel_id=1, source_target_pairs={{0,6},{1,7},{2,4},{3,5},{4,2},{5,3},{6,0},{7,1},{8,14},{9,15},{10,... | collective-permute-start | bytes 196616 | tf_op jit(solution)/shard_map/ppermute | solution.py:37

commit v2 on v1

v2 whole, which is shorter than its diff:
```python
import functools

import jax
import jax.numpy as jnp
from jax import lax
from jax.experimental import pallas as pl
from jax.experimental.pallas import tpu as pltpu
from jax.sharding import PartitionSpec as P

F32, BF16 = jnp.float32, jnp.bfloat16
MIB = 1 << 20
VMEM = pl.BlockSpec(memory_space=pltpu.VMEM)
FIRST = 4
SLOTS = 4


def params(mib=12):
    return pltpu.CompilerParams(vmem_limit_bytes=mib * MIB)


def cost(flops, moved):
    return pl.CostEstimate(flops=int(flops), bytes_accessed=int(moved), transcendentals=0)


def fit(size, block):
    while size % block:
        block //= 2
    return block


def halves(value):
    high = value.astype(BF16)
    return high, (value - high.astype(F32)).astype(BF16)


def swap(value, axis, mask):
    size = lax.axis_size(axis)
    return lax.ppermute(value, axis, [(i, i ^ mask) for i in range(size)])


def load_kernel(n_mp, first, with_pre, w_ref, *refs):
    if with_pre:
        x_ref, refs = refs[0], refs[1:]
    high_ref, low_ref, refs = refs[0], refs[1], refs[2:]
    outs, refs = refs[: len(refs) - 3 if with_pre else 0], refs[-3:] if with_pre else refs[-2:]
    slots, sems = refs[0], refs[1]
    n_slot, block, count = slots.shape
    steps = high_ref.shape[0] // block

    def copy(i, slot):
        at = pl.ds(pl.multiple_of(i * block, block), block)
        return pltpu.make_async_copy(w_ref.at[at, pl.ds(first, count)], slots.at[slot], sems.at[slot])

    for i in range(min(n_slot, steps)):
        copy(i, i).start()
    if with_pre:
        total = refs[2]
        rows = total.shape[0]
        total[...] = jnp.zeros_like(total)

    def step(i, _):
        slot = lax.rem(i, n_slot)
        at = pl.ds(pl.multiple_of(i * block, block), block)
        copy(i, slot).wait()
        high, low = halves(slots[slot])
        high_ref[at, :] = high
        low_ref[at, :] = low

        @pl.when(i + n_slot < steps)
        def _():
            copy(i + n_slot, slot).start()

        if with_pre:
            total[...] += product(x_ref, high_ref, low_ref, at, slice(None))
        return 0

    lax.fori_loop(0, steps, step, 0)
    if with_pre:
        group = rows // n_mp
        for mask in range(n_mp):
            outs[mask][...] = total[mask * group : (mask + 1) * group]


def product(x_ref, high_ref, low_ref, deep, cols):
    rows = x_ref.shape[0] // 2
    both = jnp.dot(x_ref[:, deep], high_ref[deep, cols], preferred_element_type=F32)
    last = jnp.dot(x_ref[:rows, deep], low_ref[deep, cols], preferred_element_type=F32)
    return both[:rows] + both[rows:] + last


def load_weight(weight, first, count, n_mp, x=None):
    deep = weight.shape[0]
    block = fit(deep, 256)
    ins, shapes = [weight], [pltpu.VMEM((deep, count), BF16)] * 2
    specs = [pl.BlockSpec(memory_space=pl.ANY)]
    scratch = [pltpu.VMEM((min(SLOTS, deep // block), block, count), F32), pltpu.SemaphoreType.DMA((SLOTS,))]
    if x is not None:
        rows = x.shape[0] // 2
        ins, specs = ins + [x], specs + [VMEM]
        shapes = shapes + [jax.ShapeDtypeStruct((rows // n_mp, count), F32)] * n_mp
        scratch = scratch + [pltpu.VMEM((rows, count), F32)]
    out = pl.pallas_call(
        functools.partial(load_kernel, n_mp, first, x is not None),
        in_specs=specs,
        out_specs=[VMEM] * len(shapes),
        out_shape=shapes,
        scratch_shapes=scratch,
        compiler_params=params(14),
        cost_estimate=cost(0, 4 * deep * count),
        name="load_weight",
    )(*ins)
    return out[0], out[1], out[2:]


def lay_kernel(*refs):
    refs = refs[1:]
    size = refs[0].shape[0]
    for mask, ref in enumerate(refs[:-1]):
        refs[-1][mask * size : (mask + 1) * size, :] = ref[...]


def lay_rows(pieces, after):
    size, deep = pieces[0].shape
    return pl.pallas_call(
        lay_kernel,
        in_specs=[pl.BlockSpec(memory_space=pl.ANY)] + [VMEM] * len(pieces),
        out_specs=VMEM,
        out_shape=jax.ShapeDtypeStruct((size * len(pieces), deep), F32),
        compiler_params=params(),
        cost_estimate=cost(0, 8 * size * len(pieces) * deep),
        name="lay_rows",
    )(after, *pieces)


def rows_kernel(n_mp, size, own_ref, other_ref, x_ref, flat):
    rows = flat.shape[0]
    hid = lax.axis_index("hidden")
    me = lax.axis_index("mp")
    for mask in range(rows // size // 2):
        own = hid ^ (2 * mask)
        at = slice(mask * size, (mask + 1) * size)
        flat[pl.ds(pl.multiple_of(own * size, size), size), :] = own_ref[at, :]
        flat[pl.ds(pl.multiple_of((own ^ 1) * size, size), size), :] = other_ref[at, :]
    group = rows // n_mp
    for mask in range(n_mp):
        block = flat[pl.ds(pl.multiple_of((me ^ mask) * group, group), group), :]
        high, low = halves(block)
        x_ref[mask * group : (mask + 1) * group, :] = high
        x_ref[rows + mask * group : rows + (mask + 1) * group, :] = low


def order_rows(own, other, n_mp, size):
    rows, deep = 2 * own.shape[0], own.shape[1]
    return pl.pallas_call(
        functools.partial(rows_kernel, n_mp, size),
        in_specs=[VMEM] * 2,
        out_specs=VMEM,
        out_shape=jax.ShapeDtypeStruct((2 * rows, deep), BF16),
        scratch_shapes=[pltpu.VMEM((rows, deep), F32)],
        compiler_params=params(),
        cost_estimate=cost(0, 8 * rows * deep),
        name="order_rows",
    )(own, other)


def turn_kernel(x_ref, t_ref):
    rows = x_ref.shape[0] // 2
    high = x_ref[:rows, :].astype(F32)
    low = x_ref[rows:, :].astype(F32)
    t_ref[...] = jnp.concatenate([high, high, low, low], axis=0).T.astype(BF16)


def turn_rows(x):
    two, deep = x.shape
    return pl.pallas_call(
        turn_kernel,
        in_specs=[VMEM],
        out_specs=VMEM,
        out_shape=jax.ShapeDtypeStruct((deep, 2 * two), BF16),
        compiler_params=params(),
        cost_estimate=cost(0, 4 * two * deep),
        name="turn_rows",
    )(x)


def pre_kernel(n_mp, block, x_ref, high_ref, low_ref, *outs):
    group = x_ref.shape[0] // 2 // n_mp

    def step(j, _):
        here = pl.ds(pl.multiple_of(j * block, block), block)
        total = product(x_ref, high_ref, low_ref, slice(None), here)
        for mask in range(n_mp):
            outs[mask][:, here] = total[mask * group : (mask + 1) * group]
        return 0

    lax.fori_loop(0, outs[0].shape[1] // block, step, 0)


def partial_pre(x, high, low, n_mp):
    rows, deep, count = x.shape[0] // 2, x.shape[1], high.shape[1]
    return pl.pallas_call(
        functools.partial(pre_kernel, n_mp, fit(count, 512)),
        in_specs=[VMEM] * 3,
        out_specs=[VMEM] * n_mp,
        out_shape=[jax.ShapeDtypeStruct((rows // n_mp, count), F32)] * n_mp,
        compiler_params=params(),
        cost_estimate=cost(20 * rows * deep * count, 4 * rows * count),
        name="partial_pre",
    )(x, high, low)


def slope_kernel(first, *refs):
    parts, up_ref, out_ref = refs[:-2], refs[-2], refs[-1]
    pre = parts[0][...]
    for part in parts[1:]:
        pre = pre + part[...]
    cdf = 0.5 * (1.0 + lax.erf(pre * 0.7071067811865476))
    slope = cdf + pre * jnp.exp(-0.5 * pre * pre) * 0.3989422804014327
    out_ref[...] = up_ref[:, first : first + pre.shape[1]] * slope


def grad_mine(parts, upstream, first):
    rows, count = parts[0].shape
    return pl.pallas_call(
        functools.partial(slope_kernel, first),
        in_specs=[VMEM] * (len(parts) + 1),
        out_specs=VMEM,
        out_shape=jax.ShapeDtypeStruct((rows, count), F32),
        compiler_params=params(),
        cost_estimate=cost(0, 24 * rows * count),
        name="grad_mine",
    )(*parts, upstream)


def stacked(pieces):
    return halves(jnp.concatenate([piece[...] for piece in pieces], axis=0))


def grads_kernel(n_mp, block, first, do_input, is_last, do_weight, n_skip, *refs):
    refs = list(refs)

    def take(n):
        head = refs[:n]
        del refs[:n]
        return head

    if do_input:
        high_ref, low_ref = take(2)
        in_pieces = take(n_mp)
        (total_ref,) = take(1) if do_input == 2 else (None,)
    if do_weight:
        (t_ref,) = take(1)
        weight_pieces = take(n_mp)
        take(n_skip)
    if do_input:
        outs = take(2 if is_last else 1)
    if do_weight:
        (out_ref,) = take(1)
    if do_input:
        stack_in, flat = take(2)
    if do_weight:
        slots, sems, stack_weight = take(3)
        n_slot, count = slots.shape[0], slots.shape[2]

    steps = (high_ref if do_input else t_ref).shape[0] // block
    if do_weight:
        high, low = stacked(weight_pieces)
        stack_weight[...] = jnp.concatenate([high, low, high, low], axis=0)
    if do_input:
        high, low = stacked(in_pieces)
        stack_in[...] = jnp.concatenate([high.astype(F32), low.astype(F32)], axis=0).T.astype(BF16)
        rows = high.shape[0]
        group = rows // n_mp
        me = lax.axis_index("mp")
        hid = lax.axis_index("hidden")

    def copy(i, slot):
        at = pl.ds(pl.multiple_of(i * block, block), block)
        return pltpu.make_async_copy(slots.at[slot], out_ref.at[at, pl.ds(first, count)], sems.at[slot])

    def step(i, _):
        here = pl.ds(pl.multiple_of(i * block, block), block)
        if do_weight:
            slot = lax.rem(i, n_slot)

            @pl.when(i >= n_slot)
            def _():
                copy(i - n_slot, slot).wait()

            slots[slot] = jnp.dot(t_ref[here, :], stack_weight[...], preferred_element_type=F32)
            copy(i, slot).start()
        if do_input:
            both = jnp.dot(high_ref[here, :], stack_in[...], preferred_element_type=F32)
            last = jnp.dot(low_ref[here, :], stack_in[:, :rows], preferred_element_type=F32)
            total = (both[:, :rows] + both[:, rows:] + last).T
            if total_ref is not None:
                total = total + total_ref[:, here]
            if not is_last:
                outs[0][:, here] = total
                return 0
            for mask in range(n_mp):
                place = pl.ds(pl.multiple_of((me ^ mask) * group, group), group)
                flat[place, :] = total[mask * group : (mask + 1) * group]
            keep_ref, send_ref = outs
            n_pair, size = keep_ref.shape[0], keep_ref.shape[1]
            for mask in range(n_pair):
                own = hid ^ (2 * mask)
                keep_ref[mask, :, here] = flat[pl.ds(pl.multiple_of(own * size, size), size), :]
                other = own ^ 1
                send_ref[mask, :, here] = flat[pl.ds(pl.multiple_of(other * size, size), size), :]
        return 0

    lax.fori_loop(0, steps, step, 0)
    if do_weight:
        for i in range(max(0, steps - n_slot), steps):
            copy(i, i % n_slot).wait()


def grads(n_hid, input_part=None, is_last=False, weight_part=None):
    ins, specs, shapes, outs, scratch, aliases = [], [], [], [], [], {}
    hbm = pl.BlockSpec(memory_space=pl.ANY)
    first = n_skip = do_input = 0
    if input_part is not None:
        high, low, pieces, total = input_part
        n_mp, (group, count) = len(pieces), pieces[0].shape
        rows, deep = group * n_mp, high.shape[0]
        do_input = 1 if total is None else 2
        ins += [high, low, *pieces] + ([] if total is None else [total])
        specs += [VMEM] * len(ins)
        if is_last:
            shapes += [jax.ShapeDtypeStruct((n_hid // 2, rows // n_hid, deep), F32)] * 2
        else:
            shapes += [jax.ShapeDtypeStruct((rows, deep), F32)]
        outs += [VMEM] * len(shapes)
        block = fit(deep, 256 if weight_part else 512)
        scratch += [pltpu.VMEM((count, 2 * rows), BF16), pltpu.VMEM((rows, block), F32)]
    if weight_part is not None:
        turned, pieces, base, first, wide = weight_part
        n_mp, (group, count) = len(pieces), pieces[0].shape
        rows, deep = group * n_mp, turned.shape[0]
        block = fit(deep, 256)
        slots = min(3, deep // block)
        ins += [turned, *pieces]
        specs += [VMEM] * (n_mp + 1)
        if base is not None:
            aliases = {len(ins): len(shapes)}
            ins, specs, n_skip = ins + [base], specs + [hbm], 1
        shapes += [jax.ShapeDtypeStruct((deep, wide), F32)]
        outs += [hbm]
        scratch += [
            pltpu.VMEM((slots, block, count), F32),
            pltpu.SemaphoreType.DMA((slots,)),
            pltpu.VMEM((4 * rows, count), BF16),
        ]
    return pl.pallas_call(
        functools.partial(grads_kernel, n_mp, block, first, do_input, is_last, weight_part is not None, n_skip),
        in_specs=specs,
        out_specs=outs,
        out_shape=shapes,
        scratch_shapes=scratch,
        input_output_aliases=aliases,
        compiler_params=params(14),
        cost_estimate=cost(0, 4 * deep * count),
        name="grads",
    )(*ins)


def pair_kernel(*refs):
    keep_ref, got_ref, outs = refs[0], refs[1], refs[2:]
    for mask in range(len(outs)):
        outs[mask][...] = keep_ref[mask] + got_ref[mask]


def pair_sums(keep, got):
    n, size, deep = keep.shape
    return pl.pallas_call(
        pair_kernel,
        in_specs=[VMEM] * 2,
        out_specs=[VMEM] * n,
        out_shape=[jax.ShapeDtypeStruct((size, deep), F32)] * n,
        compiler_params=params(),
        cost_estimate=cost(0, 12 * n * size * deep),
        name="pair_sums",
    )(keep, got)


def add_kernel(*refs):
    total = refs[0][...]
    for ref in refs[1:-1]:
        total = total + ref[...]
    refs[-1][...] = total


def add_up(parts):
    return pl.pallas_call(
        add_kernel,
        in_specs=[VMEM] * len(parts),
        out_specs=VMEM,
        out_shape=jax.ShapeDtypeStruct(parts[0].shape, F32),
        compiler_params=params(),
        name="add_up",
    )(*parts)


def body(inputs, weight, upstream):
    n_mp, n_hid = lax.axis_size("mp"), lax.axis_size("hidden")
    wide = weight.shape[1]
    cut = wide * FIRST // 8
    ranges = [(0, cut), (cut, wide - cut)]

    high_a, low_a, _ = load_weight(weight, *ranges[0], n_mp)
    own = lay_rows([inputs] + [swap(inputs, "hidden", 2 * mask) for mask in range(1, n_hid // 2)], high_a)
    x = order_rows(own, swap(own, "hidden", 1), n_mp, inputs.shape[0])
    part_a = partial_pre(x, high_a, low_a, n_mp)
    high_b, low_b, part_b = load_weight(weight, *ranges[1], n_mp, x)
    turned = turn_rows(x)

    grad = []
    for (first, _), own in zip(ranges, (part_a, part_b)):
        got = [own[0]] + [swap(own[mask], "mp", mask) for mask in range(1, n_mp)]
        mine = grad_mine(got, upstream, first)
        grad.append([mine] + [swap(mine, "mp", mask) for mask in range(1, n_mp)])

    (total,) = grads(n_hid, (high_a, low_a, grad[0], None))
    keep, send, weight_grad = grads(
        n_hid, (high_b, low_b, grad[1], total), True, (turned, grad[0], None, 0, wide)
    )
    (weight_grad,) = grads(n_hid, weight_part=(turned, grad[1], weight_grad, cut, wide))
    sums = pair_sums(keep, swap(send, "hidden", 1))
    input_grad = add_up([sums[0]] + [swap(sums[mask], "hidden", 2 * mask) for mask in range(1, n_hid // 2)])
    return input_grad, weight_grad


def solution(mesh):
    placed = (P("hidden", "mp"), P("mp", "hidden"), P("mp", "hidden"))
    return jax.shard_map(
        body,
        mesh=mesh,
        in_specs=placed,
        out_specs=(P("hidden", "mp"), P("mp", "hidden")),
        check_vma=False,
    )
```

time: 93.6 us -> 75.1 us (0.80)
  Pallas kernels: 57.8 us -> 40.2 us
    pallas_call x8, Pallas kernels: 56.6 us -> 39.1 us  [the longest x3 21.9 us: grads(): pl.pallas_call(functools.partial(grads_kernel, n_mp, block, first, do_inp...]
  transfers between devices with their start and end apart: 20 -> 20, of which waited for: 3 -> 4; matrix products, arithmetic and copies ran while one was open for 0% -> 0% of each run, Pallas kernels for 48% -> 36%
where the time goes in v2:
time: 75.1 us; the launch traced here: 75 us
  Pallas kernels  40.2 us (54%)
  starting transfers between devices  25.6 us (34%)
  waiting for transfers between devices  8.25 us (11%)
  between operations  0.85 us (1%)
    ppermute x20, starting transfers between devices, swap(): return lax.ppermute(value, axis, [(i, i ^ mask) for i in range(size)])  25.6 us
    pallas_call x3, Pallas kernels, grads(): pl.pallas_call(functools.partial(grads_kernel, n_mp, block, first, do_inp...  21.9 us
    pallas_call x2, Pallas kernels, load_weight(): pl.pallas_call(functools.partial(load_kernel, n_mp, first, x is not None)...  13.9 us
    ppermute x20, waiting for transfers between devices, swap(): return lax.ppermute(value, axis, [(i, i ^ mask) for i in range(size)])  8.25 us
    pallas_call x1, Pallas kernels, partial_pre(): pl.pallas_call(functools.partial(pre_kernel, n_mp, fit(count, 512)), in_s...  3.14 us
  transfers between devices with their start and end apart: 20, of which 4 were waited for; matrix products, arithmetic and copies ran while one was open for 0% of the time, Pallas kernels for 36%

profile of v2, /device:TPU:0, one launch (start us, length us, event | category | flops | bytes accessed | tf_op | source)
XLA Modules:
  0.0 75.0 jit_solution(15168518146802897274)
XLA Ops:
  0.6 4.1 %collective-permute-start.1 = (f32[8,2048]{1,0:T(8,128)}, f32[8,2048]{1,0:T(8,128)S(1)}, u32[]{:S(2)}, u32[]{:S(2)}) collective-permute-start(f32[8,2048]{1,0:T(8,128)} %refs_1_.1), channel_id=1, source_target_pairs={{0,4},{1,5},{2,6},{3,7},{4,0},{5,1},{6,2},{7,3},{8,12},{9,13},{10,... | collective-permute-start | bytes 196616 | tf_op jit(solution)/shard_map/ppermute | solution.py:38
  4.7 1.6 %collective-permute-start = (f32[8,2048]{1,0:T(8,128)}, f32[8,2048]{1,0:T(8,128)S(1)}, u32[]{:S(2)}, u32[]{:S(2)}) collective-permute-start(f32[8,2048]{1,0:T(8,128)} %refs_1_.1), channel_id=1, source_target_pairs={{0,2},{1,3},{2,0},{3,1},{4,6},{5,7},{6,4},{7,5},{8,10},{9,11},{10,... | collective-permute-start | bytes 196616 | tf_op jit(solution)/shard_map/ppermute | solution.py:38
  6.3 6.4 %load_weight.2 = (bf16[2048,2048]{1,0:T(8,128)(2,1)S(1)}, bf16[2048,2048]{1,0:T(8,128)(2,1)S(1)}) custom-call(f32[2048,4096]{1,0:T(8,128)} %w_ref.3), custom_call_target="tpu_custom_call" | custom-call | bytes 16777216 | tf_op jit(solution)/shard_map/load_weight/pallas_call | solution.py:102
  12.8 0.1 collective-permute-start.3
  12.9 1.5 %collective-permute-done.3.other_ref = f32[32,2048]{1,0:T(8,128)S(1)} collective-permute-done((f32[32,2048]{1,0:T(8,128)S(1)}, f32[32,2048]{1,0:T(8,128)S(1)}, u32[]{:S(2)}, u32[]{:S(2)}) %collective-permute-start.3) | collective-permute-done | bytes 262176 | tf_op jit(solution)/shard_map/ppermute | solution.py:38
  14.4 0.1 order_rows.1.refs_0_.x_ref
  14.6 3.1 %partial_pre.1 = (f32[16,2048]{1,0:T(8,128)S(1)}, f32[16,2048]{1,0:T(8,128)S(1)}, f32[16,2048]{1,0:T(8,128)S(1)}, f32[16,2048]{1,0:T(8,128)S(1)}) custom-call(bf16[128,2048]{1,0:T(8,128)(2,1)S(1)} %order_rows.1.refs_0_.x_ref, bf16[2048,2048]{1,0:T(8,128)(2,1)S(1)} %get-tuple-element.21.refs_0_.high_ref, bf16[2048,2048]{1,0:T(8,128)(2,1)S(1)} %get-tuple-element.28.low_ref.refs_1_), custom_call_target="tpu_custom_call" | custom-call | flops 5368709120 | bytes 524288 | tf_op jit(solution)/shard_map/partial_pre/pallas_call | solution.py:201
  17.7 1.8 %collective-permute-start.10 = (f32[16,2048]{1,0:T(8,128)S(1)}, f32[16,2048]{1,0:T(8,128)S(1)}, u32[]{:S(2)}, u32[]{:S(2)}) collective-permute-start(f32[16,2048]{1,0:T(8,128)S(1)} %get-tuple-element.30), channel_id=1, source_target_pairs={{0,8},{8,0},{16,24},{24,16},{1,9},{9,1},{17,25},{25,17},{2,10},{10... | collective-permute-start | bytes 393224 | tf_op jit(solution)/shard_map/ppermute | solution.py:38
  19.5 1.5 %collective-permute-start.11 = (f32[16,2048]{1,0:T(8,128)S(1)}, f32[16,2048]{1,0:T(8,128)S(1)}, u32[]{:S(2)}, u32[]{:S(2)}) collective-permute-start(f32[16,2048]{1,0:T(8,128)S(1)} %get-tuple-element.31), channel_id=1, source_target_pairs={{0,16},{8,24},{16,0},{24,8},{1,17},{9,25},{17,1},{25,9},{2,18},{10... | collective-permute-start | bytes 393224 | tf_op jit(solution)/shard_map/ppermute | solution.py:38
  21.0 0.3 collective-permute-start.12
  21.3 7.4 %load_weight.3 = (bf16[2048,2048]{1,0:T(8,128)(2,1)S(1)}, bf16[2048,2048]{1,0:T(8,128)(2,1)S(1)}, f32[16,2048]{1,0:T(8,128)S(1)}, f32[16,2048]{1,0:T(8,128)S(1)}...) custom-call(f32[2048,4096]{1,0:T(8,128)} %w_ref.3, bf16[128,2048]{1,0:T(8,128)(2,1)S(1)} %order_rows.1.refs_0_.x_ref), custom_call_target="tpu_custom_call" | custom-call | bytes 16777216 | tf_op jit(solution)/shard_map/load_weight/pallas_call | solution.py:102
  28.7 2.0 %collective-permute-start.4 = (f32[16,2048]{1,0:T(8,128)S(1)}, f32[16,2048]{1,0:T(8,128)S(1)}, u32[]{:S(2)}, u32[]{:S(2)}) collective-permute-start(f32[16,2048]{1,0:T(8,128)S(1)} %get-tuple-element.25), channel_id=1, source_target_pairs={{0,8},{8,0},{16,24},{24,16},{1,9},{9,1},{17,25},{25,17},{2,10},{10... | collective-permute-start | bytes 393224 | tf_op jit(solution)/shard_map/ppermute | solution.py:38
  30.7 0.8 %collective-permute-start.5 = (f32[16,2048]{1,0:T(8,128)S(1)}, f32[16,2048]{1,0:T(8,128)S(1)}, u32[]{:S(2)}, u32[]{:S(2)}) collective-permute-start(f32[16,2048]{1,0:T(8,128)S(1)} %get-tuple-element.26), channel_id=1, source_target_pairs={{0,16},{8,24},{16,0},{24,8},{1,17},{9,25},{17,1},{25,9},{2,18},{10... | collective-permute-start | bytes 393224 | tf_op jit(solution)/shard_map/ppermute | solution.py:38
  31.5 0.8 %collective-permute-start.6 = (f32[16,2048]{1,0:T(8,128)S(1)}, f32[16,2048]{1,0:T(8,128)S(1)}, u32[]{:S(2)}, u32[]{:S(2)}) collective-permute-start(f32[16,2048]{1,0:T(8,128)S(1)} %get-tuple-element.27), channel_id=1, source_target_pairs={{0,24},{8,16},{16,8},{24,0},{1,25},{9,17},{17,9},{25,1},{2,26},{10... | collective-permute-start | bytes 393224 | tf_op jit(solution)/shard_map/ppermute | solution.py:38
  32.3 0.1 grad_mine.3.refs_2_.refs_8_
  32.4 2.2 %collective-permute-start.15 = (f32[16,2048]{1,0:T(8,128)S(1)}, f32[16,2048]{1,0:T(8,128)S(1)}, u32[]{:S(2)}, u32[]{:S(2)}) collective-permute-start(f32[16,2048]{1,0:T(8,128)S(1)} %grad_mine.3.refs_2_.refs_8_), channel_id=1, source_target_pairs={{0,24},{8,16},{16,8},{24,0},{1,25},{9,17},{17,9},{25,1},{2,26},{10... | collective-permute-start | bytes 393224 | tf_op jit(solution)/shard_map/ppermute | solution.py:38
  34.6 1.2 %collective-permute-start.14 = (f32[16,2048]{1,0:T(8,128)S(1)}, f32[16,2048]{1,0:T(8,128)S(1)}, u32[]{:S(2)}, u32[]{:S(2)}) collective-permute-start(f32[16,2048]{1,0:T(8,128)S(1)} %grad_mine.3.refs_2_.refs_8_), channel_id=1, source_target_pairs={{0,16},{8,24},{16,0},{24,8},{1,17},{9,25},{17,1},{25,9},{2,18},{10... | collective-permute-start | bytes 393224 | tf_op jit(solution)/shard_map/ppermute | solution.py:38
  35.8 1.3 %collective-permute-start.13 = (f32[16,2048]{1,0:T(8,128)S(1)}, f32[16,2048]{1,0:T(8,128)S(1)}, u32[]{:S(2)}, u32[]{:S(2)}) collective-permute-start(f32[16,2048]{1,0:T(8,128)S(1)} %grad_mine.3.refs_2_.refs_8_), channel_id=1, source_target_pairs={{0,8},{8,0},{16,24},{24,16},{1,9},{9,1},{17,25},{25,17},{2,10},{10... | collective-permute-start | bytes 393224 | tf_op jit(solution)/shard_map/ppermute | solution.py:38
  37.1 4.7 %collective-permute-done.5.refs_2_ = f32[16,2048]{1,0:T(8,128)S(1)} collective-permute-done((f32[16,2048]{1,0:T(8,128)S(1)}, f32[16,2048]{1,0:T(8,128)S(1)}, u32[]{:S(2)}, u32[]{:S(2)}) %collective-permute-start.5) | collective-permute-done | bytes 131104 | tf_op jit(solution)/shard_map/ppermute | solution.py:38
  41.8 0.1 grad_mine.2.refs_2_.refs_1_
  41.9 1.9 %collective-permute-start.9 = (f32[16,2048]{1,0:T(8,128)S(1)}, f32[16,2048]{1,0:T(8,128)S(1)}, u32[]{:S(2)}, u32[]{:S(2)}) collective-permute-start(f32[16,2048]{1,0:T(8,128)S(1)} %grad_mine.2.refs_2_.refs_1_), channel_id=1, source_target_pairs={{0,24},{8,16},{16,8},{24,0},{1,25},{9,17},{17,9},{25,1},{2,26},{10... | collective-permute-start | bytes 393224 | tf_op jit(solution)/shard_map/ppermute | solution.py:38
  43.8 1.7 %collective-permute-start.7 = (f32[16,2048]{1,0:T(8,128)S(1)}, f32[16,2048]{1,0:T(8,128)S(1)}, u32[]{:S(2)}, u32[]{:S(2)}) collective-permute-start(f32[16,2048]{1,0:T(8,128)S(1)} %grad_mine.2.refs_2_.refs_1_), channel_id=1, source_target_pairs={{0,8},{8,0},{16,24},{24,16},{1,9},{9,1},{17,25},{25,17},{2,10},{10... | collective-permute-start | bytes 393224 | tf_op jit(solution)/shard_map/ppermute | solution.py:38
  45.4 0.3 turn_rows.1.refs_7_.refs_0_
  45.8 0.4 collective-permute-done.14.refs_4_.refs_10_
  46.2 6.0 %grads.3.refs_6_ = f32[64,2048]{1,0:T(8,128)S(1)} custom-call(bf16[2048,2048]{1,0:T(8,128)(2,1)S(1)} %get-tuple-element.21.refs_0_.high_ref, bf16[2048,2048]{1,0:T(8,128)(2,1)S(1)} %bitcast.1, f32[16,2048]{1,0:T(8,128)S(1)} %grad_mine.3.refs_2_.refs_8_, f32[16,2048]{1,0:T(8,128)S(1)} %collective-permute-done.13.refs_3_.refs_9_, ...), custom_call_target="tpu_custom_call" | custom-call | bytes 16777216 | tf_op jit(solution)/shard_map/grads/pallas_call | solution.py:355
  52.2 9.5 %grads.4 = (f32[4,8,2048]{2,1,0:T(8,128)S(1)}, f32[4,8,2048]{2,1,0:T(8,128)S(1)}, f32[2048,4096]{1,0:T(8,128)}) custom-call(bf16[2048,2048]{1,0:T(8,128)(2,1)S(1)} %get-tuple-element.22.refs_0_, bf16[2048,2048]{1,0:T(8,128)(2,1)S(1)} %get-tuple-element.23.refs_1_, f32[16,2048]{1,0:T(8,128)S(1)} %grad_mine.2.refs_2_.refs_1_, ...), custom_call_target="tpu_custom_call" | custom-call | bytes 16777216 | tf_op jit(solution)/shard_map/grads/pallas_call | solution.py:355
  61.8 1.5 %collective-permute-done.16.refs_1_ = f32[4,8,2048]{2,1,0:T(8,128)S(1)} collective-permute-done((f32[4,8,2048]{2,1,0:T(8,128)S(1)}, f32[4,8,2048]{2,1,0:T(8,128)S(1)}, u32[]{:S(2)}, u32[]{:S(2)}) %collective-permute-start.16) | collective-permute-done | bytes 262176 | tf_op jit(solution)/shard_map/ppermute | solution.py:38
  63.4 0.7 collective-permute-start.17
  64.1 3.5 %collective-permute-start.18 = (f32[8,2048]{1,0:T(8,128)S(1)}, f32[8,2048]{1,0:T(8,128)S(1)}, u32[]{:S(2)}, u32[]{:S(2)}) collective-permute-start(f32[8,2048]{1,0:T(8,128)S(1)} %get-tuple-element.37), channel_id=1, source_target_pairs={{0,4},{1,5},{2,6},{3,7},{4,0},{5,1},{6,2},{7,3},{8,12},{9,13},{10,... | collective-permute-start | bytes 196616 | tf_op jit(solution)/shard_map/ppermute | solution.py:38
  67.5 0.3 collective-permute-start.19
  67.8 6.4 %grads.5 = f32[2048,4096]{1,0:T(8,128)} custom-call(bf16[2048,256]{1,0:T(8,128)(2,1)S(1)} %turn_rows.1.refs_7_.refs_0_, f32[16,2048]{1,0:T(8,128)S(1)} %grad_mine.2.refs_2_.refs_1_, f32[16,2048]{1,0:T(8,128)S(1)} %collective-permute-done.7.refs_3_.refs_2_, f32[16,2048]{1,0:T(8,128)S(1)} %collective-permute-done.8.refs_4_.refs_3_, ...), custom_call_target="tpu_custom_call", output_to_operand_aliasing={{}: (5, {})} | custom-call | bytes 16777216 | tf_op jit(solution)/shard_map/grads/pallas_call | solution.py:355
  74.3 0.6 add_up.1
  (32 shorter events, 0.2 us)
Async XLA Ops:
  0.6 12.2 %copy-start.2 = (f32[8,2048]{1,0:T(8,128)S(1)}, f32[8,2048]{1,0:T(8,128)}, u32[]{:S(2)}) copy-start(f32[8,2048]{1,0:T(8,128)} %refs_1_.1) | copy-start | bytes 196612
  0.6 12.1 %collective-permute-start.1 = (f32[8,2048]{1,0:T(8,128)}, f32[8,2048]{1,0:T(8,128)S(1)}, u32[]{:S(2)}, u32[]{:S(2)}) collective-permute-start(f32[8,2048]{1,0:T(8,128)} %refs_1_.1), channel_id=1, source_target_pairs={{0,4},{1,5},{2,6},{3,7},{4,0},{5,1},{6,2},{7,3},{8,12},{9,13},{10,... | collective-permute-start | bytes 196616 | tf_op jit(solution)/shard_map/ppermute | solution.py:38
  4.7 8.0 %collective-permute-start = (f32[8,2048]{1,0:T(8,128)}, f32[8,2048]{1,0:T(8,128)S(1)}, u32[]{:S(2)}, u32[]{:S(2)}) collective-permute-start(f32[8,2048]{1,0:T(8,128)} %refs_1_.1), channel_id=1, source_target_pairs={{0,2},{1,3},{2,0},{3,1},{4,6},{5,7},{6,4},{7,5},{8,10},{9,11},{10,... | collective-permute-start | bytes 196616 | tf_op jit(solution)/shard_map/ppermute | solution.py:38
  6.3 6.5 %collective-permute-start.2 = (f32[8,2048]{1,0:T(8,128)}, f32[8,2048]{1,0:T(8,128)S(1)}, u32[]{:S(2)}, u32[]{:S(2)}) collective-permute-start(f32[8,2048]{1,0:T(8,128)} %refs_1_.1), channel_id=1, source_target_pairs={{0,6},{1,7},{2,4},{3,5},{4,2},{5,3},{6,0},{7,1},{8,14},{9,15},{10,... | collective-permute-start | bytes 196616 | tf_op jit(solution)/shard_map/ppermute | solution.py:38
  12.8 5.0 %copy-start = (bf16[2048,2048]{1,0:T(8,128)(2,1)}, bf16[2048,2048]{1,0:T(8,128)(2,1)S(1)}, u32[]{:S(2)}) copy-start(bf16[2048,2048]{1,0:T(8,128)(2,1)S(1)} %get-tuple-element.28.low_ref.refs_1_) | copy-start | bytes 25165828
  12.8 1.6 %collective-permute-start.3 = (f32[32,2048]{1,0:T(8,128)S(1)}, f32[32,2048]{1,0:T(8,128)S(1)}, u32[]{:S(2)}, u32[]{:S(2)}) collective-permute-start(f32[32,2048]{1,0:T(8,128)S(1)} %lay_rows.1.own_ref), channel_id=1, source_target_pairs={{0,1},{1,0},{2,3},{3,2},{4,5},{5,4},{6,7},{7,6},{8,9},{9,8},{10,11... | collective-permute-start | bytes 786440 | tf_op jit(solution)/shard_map/ppermute | solution.py:38
  17.7 13.7 %collective-permute-start.10 = (f32[16,2048]{1,0:T(8,128)S(1)}, f32[16,2048]{1,0:T(8,128)S(1)}, u32[]{:S(2)}, u32[]{:S(2)}) collective-permute-start(f32[16,2048]{1,0:T(8,128)S(1)} %get-tuple-element.30), channel_id=1, source_target_pairs={{0,8},{8,0},{16,24},{24,16},{1,9},{9,1},{17,25},{25,17},{2,10},{10... | collective-permute-start | bytes 393224 | tf_op jit(solution)/shard_map/ppermute | solution.py:38
  19.5 12.8 %collective-permute-start.11 = (f32[16,2048]{1,0:T(8,128)S(1)}, f32[16,2048]{1,0:T(8,128)S(1)}, u32[]{:S(2)}, u32[]{:S(2)}) collective-permute-start(f32[16,2048]{1,0:T(8,128)S(1)} %get-tuple-element.31), channel_id=1, source_target_pairs={{0,16},{8,24},{16,0},{24,8},{1,17},{9,25},{17,1},{25,9},{2,18},{10... | collective-permute-start | bytes 393224 | tf_op jit(solution)/shard_map/ppermute | solution.py:38
  21.0 25.2 %slice-start = ((s8[8388608]{0:T(1024)(128)(4,1)}), s8[4194304]{0:T(1024)(128)(4,1)S(1)}, s32[]{:S(2)}) async-start(s8[8388608]{0:T(1024)(128)(4,1)} %bitcast), calls=%async_computation | async-start | bytes 8388608
  21.0 11.3 %copy-start.1 = (f32[16,4096]{1,0:T(8,128)S(1)}, f32[16,4096]{1,0:T(8,128)}, u32[]{:S(2)}) copy-start(f32[16,4096]{1,0:T(8,128)} %refs_4_.3) | copy-start | bytes 786436
  21.0 25.2 %slice-start.1 = ((s8[8388608]{0:T(1024)(128)(4,1)}), s8[4194304]{0:T(1024)(128)(4,1)S(1)}, s32[]{:S(2)}) async-start(s8[8388608]{0:T(1024)(128)(4,1)} %bitcast), calls=%async_computation.1 | async-start | bytes 8388608
  21.0 11.3 %collective-permute-start.12 = (f32[16,2048]{1,0:T(8,128)S(1)}, f32[16,2048]{1,0:T(8,128)S(1)}, u32[]{:S(2)}, u32[]{:S(2)}) collective-permute-start(f32[16,2048]{1,0:T(8,128)S(1)} %get-tuple-element.32), channel_id=1, source_target_pairs={{0,24},{8,16},{16,8},{24,0},{1,25},{9,17},{17,9},{25,1},{2,26},{10... | collective-permute-start | bytes 393224 | tf_op jit(solution)/shard_map/ppermute | solution.py:38
  28.7 7.1 %collective-permute-start.4 = (f32[16,2048]{1,0:T(8,128)S(1)}, f32[16,2048]{1,0:T(8,128)S(1)}, u32[]{:S(2)}, u32[]{:S(2)}) collective-permute-start(f32[16,2048]{1,0:T(8,128)S(1)} %get-tuple-element.25), channel_id=1, source_target_pairs={{0,8},{8,0},{16,24},{24,16},{1,9},{9,1},{17,25},{25,17},{2,10},{10... | collective-permute-start | bytes 393224 | tf_op jit(solution)/shard_map/ppermute | solution.py:38
  30.7 11.1 %collective-permute-start.5 = (f32[16,2048]{1,0:T(8,128)S(1)}, f32[16,2048]{1,0:T(8,128)S(1)}, u32[]{:S(2)}, u32[]{:S(2)}) collective-permute-start(f32[16,2048]{1,0:T(8,128)S(1)} %get-tuple-element.26), channel_id=1, source_target_pairs={{0,16},{8,24},{16,0},{24,8},{1,17},{9,25},{17,1},{25,9},{2,18},{10... | collective-permute-start | bytes 393224 | tf_op jit(solution)/shard_map/ppermute | solution.py:38
  31.5 10.3 %collective-permute-start.6 = (f32[16,2048]{1,0:T(8,128)S(1)}, f32[16,2048]{1,0:T(8,128)S(1)}, u32[]{:S(2)}, u32[]{:S(2)}) collective-permute-start(f32[16,2048]{1,0:T(8,128)S(1)} %get-tuple-element.27), channel_id=1, source_target_pairs={{0,24},{8,16},{16,8},{24,0},{1,25},{9,17},{17,9},{25,1},{2,26},{10... | collective-permute-start | bytes 393224 | tf_op jit(solution)/shard_map/ppermute | solution.py:38
  32.4 11.4 %collective-permute-start.15 = (f32[16,2048]{1,0:T(8,128)S(1)}, f32[16,2048]{1,0:T(8,128)S(1)}, u32[]{:S(2)}, u32[]{:S(2)}) collective-permute-start(f32[16,2048]{1,0:T(8,128)S(1)} %grad_mine.3.refs_2_.refs_8_), channel_id=1, source_target_pairs={{0,24},{8,16},{16,8},{24,0},{1,25},{9,17},{17,9},{25,1},{2,26},{10... | collective-permute-start | bytes 393224 | tf_op jit(solution)/shard_map/ppermute | solution.py:38
  34.6 11.7 %collective-permute-start.14 = (f32[16,2048]{1,0:T(8,128)S(1)}, f32[16,2048]{1,0:T(8,128)S(1)}, u32[]{:S(2)}, u32[]{:S(2)}) collective-permute-start(f32[16,2048]{1,0:T(8,128)S(1)} %grad_mine.3.refs_2_.refs_8_), channel_id=1, source_target_pairs={{0,16},{8,24},{16,0},{24,8},{1,17},{9,25},{17,1},{25,9},{2,18},{10... | collective-permute-start | bytes 393224 | tf_op jit(solution)/shard_map/ppermute | solution.py:38
  35.8 10.4 %collective-permute-start.13 = (f32[16,2048]{1,0:T(8,128)S(1)}, f32[16,2048]{1,0:T(8,128)S(1)}, u32[]{:S(2)}, u32[]{:S(2)}) collective-permute-start(f32[16,2048]{1,0:T(8,128)S(1)} %grad_mine.3.refs_2_.refs_8_), channel_id=1, source_target_pairs={{0,8},{8,0},{16,24},{24,16},{1,9},{9,1},{17,25},{25,17},{2,10},{10... | collective-permute-start | bytes 393224 | tf_op jit(solution)/shard_map/ppermute | solution.py:38
  41.9 10.3 %collective-permute-start.9 = (f32[16,2048]{1,0:T(8,128)S(1)}, f32[16,2048]{1,0:T(8,128)S(1)}, u32[]{:S(2)}, u32[]{:S(2)}) collective-permute-start(f32[16,2048]{1,0:T(8,128)S(1)} %grad_mine.2.refs_2_.refs_1_), channel_id=1, source_target_pairs={{0,24},{8,16},{16,8},{24,0},{1,25},{9,17},{17,9},{25,1},{2,26},{10... | collective-permute-start | bytes 393224 | tf_op jit(solution)/shard_map/ppermute | solution.py:38
  43.8 8.5 %collective-permute-start.8 = (f32[16,2048]{1,0:T(8,128)S(1)}, f32[16,2048]{1,0:T(8,128)S(1)}, u32[]{:S(2)}, u32[]{:S(2)}) collective-permute-start(f32[16,2048]{1,0:T(8,128)S(1)} %grad_mine.2.refs_2_.refs_1_), channel_id=1, source_target_pairs={{0,16},{8,24},{16,0},{24,8},{1,17},{9,25},{17,1},{25,9},{2,18},{10... | collective-permute-start | bytes 393224 | tf_op jit(solution)/shard_map/ppermute | solution.py:38
  43.8 8.5 %collective-permute-start.7 = (f32[16,2048]{1,0:T(8,128)S(1)}, f32[16,2048]{1,0:T(8,128)S(1)}, u32[]{:S(2)}, u32[]{:S(2)}) collective-permute-start(f32[16,2048]{1,0:T(8,128)S(1)} %grad_mine.2.refs_2_.refs_1_), channel_id=1, source_target_pairs={{0,8},{8,0},{16,24},{24,16},{1,9},{9,1},{17,25},{25,17},{2,10},{10... | collective-permute-start | bytes 393224 | tf_op jit(solution)/shard_map/ppermute | solution.py:38
  61.8 1.6 %collective-permute-start.16 = (f32[4,8,2048]{2,1,0:T(8,128)S(1)}, f32[4,8,2048]{2,1,0:T(8,128)S(1)}, u32[]{:S(2)}, u32[]{:S(2)}) collective-permute-start(f32[4,8,2048]{2,1,0:T(8,128)S(1)} %get-tuple-element.34), channel_id=1, source_target_pairs={{0,1},{1,0},{2,3},{3,2},{4,5},{5,4},{6,7},{7,6},{8,9},{9,8},{10,11... | collective-permute-start | bytes 786440 | tf_op jit(solution)/shard_map/ppermute | solution.py:38
  63.4 10.9 %collective-permute-start.17 = (f32[8,2048]{1,0:T(8,128)S(1)}, f32[8,2048]{1,0:T(8,128)S(1)}, u32[]{:S(2)}, u32[]{:S(2)}) collective-permute-start(f32[8,2048]{1,0:T(8,128)S(1)} %get-tuple-element.36), channel_id=1, source_target_pairs={{0,2},{1,3},{2,0},{3,1},{4,6},{5,7},{6,4},{7,5},{8,10},{9,11},{10,... | collective-permute-start | bytes 196616 | tf_op jit(solution)/shard_map/ppermute | solution.py:38
  64.1 10.2 %collective-permute-start.18 = (f32[8,2048]{1,0:T(8,128)S(1)}, f32[8,2048]{1,0:T(8,128)S(1)}, u32[]{:S(2)}, u32[]{:S(2)}) collective-permute-start(f32[8,2048]{1,0:T(8,128)S(1)} %get-tuple-element.37), channel_id=1, source_target_pairs={{0,4},{1,5},{2,6},{3,7},{4,0},{5,1},{6,2},{7,3},{8,12},{9,13},{10,... | collective-permute-start | bytes 196616 | tf_op jit(solution)/shard_map/ppermute | solution.py:38
  67.5 6.8 %collective-permute-start.19 = (f32[8,2048]{1,0:T(8,128)S(1)}, f32[8,2048]{1,0:T(8,128)S(1)}, u32[]{:S(2)}, u32[]{:S(2)}) collective-permute-start(f32[8,2048]{1,0:T(8,128)S(1)} %get-tuple-element.38), channel_id=1, source_target_pairs={{0,6},{1,7},{2,4},{3,5},{4,2},{5,3},{6,0},{7,1},{8,14},{9,15},{10,... | collective-permute-start | bytes 196616 | tf_op jit(solution)/shard_map/ppermute | solution.py:38

commit v3 on v1

v3 whole, which is shorter than its diff:
```python
import functools

import jax
import jax.numpy as jnp
from jax import lax
from jax.experimental import pallas as pl
from jax.experimental.pallas import tpu as pltpu
from jax.sharding import PartitionSpec as P

F32, BF16 = jnp.float32, jnp.bfloat16
MIB = 1 << 20
VMEM = pl.BlockSpec(memory_space=pltpu.VMEM)
SLOTS = 6
EARLY = 4


def params(mib=12):
    return pltpu.CompilerParams(vmem_limit_bytes=mib * MIB)


def cost(flops, moved):
    return pl.CostEstimate(flops=int(flops), bytes_accessed=int(moved), transcendentals=0)


def fit(size, block):
    while size % block:
        block //= 2
    return block


def halves(value):
    high = value.astype(BF16)
    return high, (value - high.astype(F32)).astype(BF16)


def swap(value, axis, mask):
    size = lax.axis_size(axis)
    return lax.ppermute(value, axis, [(i, i ^ mask) for i in range(size)])


def block_copy(w_ref, held_ref, sems, first, block):
    def copy(i):
        at = pl.ds(pl.multiple_of(i * block, block), block)
        return pltpu.make_async_copy(w_ref.at[at, pl.ds(first, held_ref.shape[1])], held_ref.at[at, :], sems.at[i])

    return copy


def load_kernel(first, block, w_ref, held_ref, sems):
    copy = block_copy(w_ref, held_ref, sems, first, block)
    steps = held_ref.shape[0] // block
    for i in range(steps):
        copy(i).start()
    for i in range(steps):
        copy(i).wait()


def load_weight(weight, first, count):
    deep = weight.shape[0]
    block = fit(deep, 256)
    return pl.pallas_call(
        functools.partial(load_kernel, first, block),
        in_specs=[pl.BlockSpec(memory_space=pl.ANY)],
        out_specs=VMEM,
        out_shape=pltpu.VMEM((deep, count), F32),
        scratch_shapes=[pltpu.SemaphoreType.DMA((deep // block,))],
        compiler_params=params(),
        cost_estimate=cost(0, 4 * deep * count),
        name="load_weight",
    )(weight)


def product(x_ref, w_ref, deep, at, cols=slice(None)):
    rows = x_ref.shape[0] // 2
    high, low = halves(w_ref[at, cols])
    both = jnp.dot(x_ref[:, deep], high, preferred_element_type=F32)
    last = jnp.dot(x_ref[:rows, deep], low, preferred_element_type=F32)
    return both[:rows] + both[rows:] + last


def lay_kernel(*refs):
    refs = refs[1:]
    size = refs[0].shape[0]
    for mask, ref in enumerate(refs[:-1]):
        refs[-1][mask * size : (mask + 1) * size, :] = ref[...]


def lay_rows(pieces, after):
    size, deep = pieces[0].shape
    return pl.pallas_call(
        lay_kernel,
        in_specs=[pl.BlockSpec(memory_space=pl.ANY)] + [VMEM] * len(pieces),
        out_specs=VMEM,
        out_shape=jax.ShapeDtypeStruct((size * len(pieces), deep), F32),
        compiler_params=params(),
        cost_estimate=cost(0, 8 * size * len(pieces) * deep),
        name="lay_rows",
    )(after, *pieces)


def rows_kernel(n_mp, size, own_ref, other_ref, x_ref, flat):
    rows = flat.shape[0]
    hid = lax.axis_index("hidden")
    me = lax.axis_index("mp")
    for mask in range(rows // size // 2):
        own = hid ^ (2 * mask)
        at = slice(mask * size, (mask + 1) * size)
        flat[pl.ds(pl.multiple_of(own * size, size), size), :] = own_ref[at, :]
        flat[pl.ds(pl.multiple_of((own ^ 1) * size, size), size), :] = other_ref[at, :]
    group = rows // n_mp
    for mask in range(n_mp):
        block = flat[pl.ds(pl.multiple_of((me ^ mask) * group, group), group), :]
        high, low = halves(block)
        x_ref[mask * group : (mask + 1) * group, :] = high
        x_ref[rows + mask * group : rows + (mask + 1) * group, :] = low


def order_rows(own, other, n_mp, size):
    rows, deep = 2 * own.shape[0], own.shape[1]
    return pl.pallas_call(
        functools.partial(rows_kernel, n_mp, size),
        in_specs=[VMEM] * 2,
        out_specs=VMEM,
        out_shape=jax.ShapeDtypeStruct((2 * rows, deep), BF16),
        scratch_shapes=[pltpu.VMEM((rows, deep), F32)],
        compiler_params=params(),
        cost_estimate=cost(0, 8 * rows * deep),
        name="order_rows",
    )(own, other)


def turn_kernel(x_ref, t_ref):
    rows = x_ref.shape[0] // 2
    high = x_ref[:rows, :].astype(F32)
    low = x_ref[rows:, :].astype(F32)
    t_ref[...] = jnp.concatenate([high, high, low, low], axis=0).T.astype(BF16)


def turn_rows(x):
    two, deep = x.shape
    return pl.pallas_call(
        turn_kernel,
        in_specs=[VMEM],
        out_specs=VMEM,
        out_shape=jax.ShapeDtypeStruct((deep, 2 * two), BF16),
        compiler_params=params(),
        cost_estimate=cost(0, 4 * two * deep),
        name="turn_rows",
    )(x)


def first_kernel(n_mp, block, first, piece, x_ref, w_ref, all_ref, *refs):
    outs, held_ref, sems = refs[:n_mp], refs[n_mp], refs[n_mp + 1]
    group = x_ref.shape[0] // 2 // n_mp
    copy = block_copy(all_ref, held_ref, sems, first, piece)
    loads = sems.shape[0]
    for i in range(loads):
        copy(i).start()

    def step(j, _):
        here = pl.ds(pl.multiple_of(j * block, block), block)
        total = product(x_ref, w_ref, slice(None), slice(None), here)
        for mask in range(n_mp):
            outs[mask][:, here] = total[mask * group : (mask + 1) * group]
        return 0

    lax.fori_loop(0, outs[0].shape[1] // block, step, 0)
    for i in range(loads):
        copy(i).wait()


def second_kernel(n_mp, first, piece, x_ref, old_ref, all_ref, *refs):
    outs, held_ref, sems, total = refs[:n_mp], refs[n_mp], refs[n_mp + 1], refs[n_mp + 2]
    half = old_ref.shape[0]
    copy = block_copy(all_ref.at[pl.ds(half, held_ref.shape[0]), :], held_ref, sems, first, piece)
    for i in range(sems.shape[0]):
        copy(i).start()
    total[...] = jnp.zeros_like(total)

    def add(base, ref, i):
        at = pl.ds(pl.multiple_of(i * piece, piece), piece)
        deep = pl.ds(pl.multiple_of(base + i * piece, piece), piece)
        total[...] += product(x_ref, ref, deep, at)

    def old_step(i, _):
        add(0, old_ref, i)
        return 0

    def new_step(i, _):
        copy(i).wait()
        add(half, held_ref, i)
        return 0

    lax.fori_loop(0, half // piece, old_step, 0)
    lax.fori_loop(0, held_ref.shape[0] // piece, new_step, 0)
    group = total.shape[0] // n_mp
    for mask in range(n_mp):
        outs[mask][...] = total[mask * group : (mask + 1) * group]


def partial_pre(x, held, weight, first, count, n_mp, is_first):
    rows, deep = x.shape[0] // 2, x.shape[1]
    half = deep // 2
    piece = fit(half, 256)
    width = held.shape[1] if is_first else count
    scratch = [pltpu.SemaphoreType.DMA((half // piece,))]
    if is_first:
        kernel = functools.partial(first_kernel, n_mp, fit(width, 256), first, piece)
    else:
        kernel = functools.partial(second_kernel, n_mp, first, piece)
        scratch = scratch + [pltpu.VMEM((rows, count), F32)]
    out = pl.pallas_call(
        kernel,
        in_specs=[VMEM, VMEM, pl.BlockSpec(memory_space=pl.ANY)],
        out_specs=[VMEM] * (n_mp + 1),
        out_shape=[jax.ShapeDtypeStruct((rows // n_mp, width), F32)] * n_mp + [pltpu.VMEM((half, count), F32)],
        scratch_shapes=scratch,
        compiler_params=params(),
        cost_estimate=cost(20 * rows * deep * width, 4 * rows * width),
        name="partial_pre",
    )(x, held, weight)
    return out[:n_mp], out[n_mp]


def slope_kernel(first, n_parts, *refs):
    parts, up_ref, refs = refs[:n_parts], refs[n_parts], refs[n_parts + 1 :]
    n_pass = len(refs) // 2
    pre = parts[0][...]
    for part in parts[1:]:
        pre = pre + part[...]
    cdf = 0.5 * (1.0 + lax.erf(pre * 0.7071067811865476))
    slope = cdf + pre * jnp.exp(-0.5 * pre * pre) * 0.3989422804014327
    refs[n_pass][...] = up_ref[:, first : first + pre.shape[1]] * slope
    for source, target in zip(refs[:n_pass], refs[n_pass + 1 :]):
        target[...] = source[...]


def grad_mine(parts, upstream, first, passed=()):
    rows, count = parts[0].shape
    out = pl.pallas_call(
        functools.partial(slope_kernel, first, len(parts)),
        in_specs=[VMEM] * (len(parts) + 1 + len(passed)),
        out_specs=[VMEM] * (1 + len(passed)),
        out_shape=[jax.ShapeDtypeStruct((rows, count), F32)] + [jax.ShapeDtypeStruct(p.shape, F32) for p in passed],
        compiler_params=params(),
        cost_estimate=cost(0, 24 * rows * count),
        name="grad_mine",
    )(*parts, upstream, *passed)
    return out[0], list(out[1:])


def stacked(pieces):
    return halves(jnp.concatenate([piece[...] for piece in pieces], axis=0))


def input_kernel(n_mp, n_weight, block, has_total, is_last, *refs):
    w_refs, pieces, refs = refs[:n_weight], refs[n_weight : n_weight + n_mp], refs[n_weight + n_mp :]
    total_ref, outs, (stack, flat) = refs[0] if has_total else None, refs[has_total:-2], refs[-2:]
    high, low = stacked(pieces)
    stack[...] = jnp.concatenate([high.astype(F32), low.astype(F32)], axis=0).T.astype(BF16)
    rows = high.shape[0]
    group = rows // n_mp
    me = lax.axis_index("mp")
    hid = lax.axis_index("hidden")

    def step(w_ref, base, i):
        here = pl.ds(pl.multiple_of(base + i * block, block), block)
        high, low = halves(w_ref[pl.ds(pl.multiple_of(i * block, block), block), :])
        both = jnp.dot(high, stack[...], preferred_element_type=F32)
        last = jnp.dot(low, stack[:, :rows], preferred_element_type=F32)
        total = (both[:, :rows] + both[:, rows:] + last).T
        if total_ref is not None:
            total = total + total_ref[:, here]
        if not is_last:
            outs[0][:, here] = total
            return 0
        for mask in range(n_mp):
            place = pl.ds(pl.multiple_of((me ^ mask) * group, group), group)
            flat[place, :] = total[mask * group : (mask + 1) * group]
        keep_ref, send_ref = outs
        n_pair, size = keep_ref.shape[0], keep_ref.shape[1]
        for mask in range(n_pair):
            own = hid ^ (2 * mask)
            keep_ref[mask, :, here] = flat[pl.ds(pl.multiple_of(own * size, size), size), :]
            other = own ^ 1
            send_ref[mask, :, here] = flat[pl.ds(pl.multiple_of(other * size, size), size), :]
        return 0

    base = 0
    for w_ref in w_refs:
        lax.fori_loop(0, w_ref.shape[0] // block, lambda i, _, w=w_ref, at=base: step(w, at, i), 0)
        base += w_ref.shape[0]


def input_share(weights, pieces, total, n_hid, is_last):
    n_mp, (group, count) = len(pieces), pieces[0].shape
    rows, deep = group * n_mp, sum(w.shape[0] for w in weights)
    block = fit(weights[0].shape[0], 1024)
    ins = [*weights, *pieces] + ([] if total is None else [total])
    if is_last:
        shapes = [jax.ShapeDtypeStruct((n_hid // 2, rows // n_hid, deep), F32)] * 2
    else:
        shapes = [jax.ShapeDtypeStruct((rows, deep), F32)]
    return pl.pallas_call(
        functools.partial(input_kernel, n_mp, len(weights), block, int(total is not None), is_last),
        in_specs=[VMEM] * len(ins),
        out_specs=[VMEM] * len(shapes),
        out_shape=shapes,
        scratch_shapes=[pltpu.VMEM((count, 2 * rows), BF16), pltpu.VMEM((rows, block), F32)],
        compiler_params=params(14),
        cost_estimate=cost(20 * rows * deep * count, 4 * rows * deep),
        name="input_share",
    )(*ins)


def weight_kernel(n_mp, part, jobs, n_skip, t_ref, *refs):
    groups, refs = [refs[j * n_mp : (j + 1) * n_mp] for j in range(len(jobs))], refs[len(jobs) * n_mp + n_skip :]
    out_ref, mark_ref, slots, sems, stacks = refs
    mark_ref[...] = jnp.zeros_like(mark_ref)
    n_slot, count = slots.shape[0], slots.shape[2]

    def copy(i, first, row):
        slot = lax.rem(i, n_slot)
        at = pl.ds(pl.multiple_of(row, part), part)
        return pltpu.make_async_copy(slots.at[slot], out_ref.at[at, pl.ds(first, count)], sems.at[slot])

    done = 0
    for j, (first, start, end) in enumerate(jobs):
        high, low = stacked(groups[j])
        stacks[j] = jnp.concatenate([high, low, high, low], axis=0)

        def step(i, _, j=j, first=first, start=start, base=done):
            turn = base + i

            @pl.when(turn >= n_slot)
            def _():
                copy(turn, first, start).wait()

            row = start + i * part
            at = pl.ds(pl.multiple_of(row, part), part)
            slots[lax.rem(turn, n_slot)] = jnp.dot(t_ref[at, :], stacks[j], preferred_element_type=F32)
            copy(turn, first, row).start()
            return 0

        lax.fori_loop(0, (end - start) // part, step, 0)
        done += (end - start) // part
    for i in range(max(0, done - n_slot), done):
        copy(i, jobs[-1][0], jobs[-1][1]).wait()


def weight_part(turned, jobs, part, base, after, wide):
    pieces = [piece for job in jobs for piece in job[0]]
    n_mp, (group, count) = len(jobs[0][0]), pieces[0].shape
    rows, deep = group * n_mp, turned.shape[0]
    skipped = [after] if base is None else [after, base]
    ins = [turned, *pieces, *skipped]
    return pl.pallas_call(
        functools.partial(weight_kernel, n_mp, part, [job[1:] for job in jobs], len(skipped)),
        in_specs=[VMEM] * (1 + len(pieces)) + [pl.BlockSpec(memory_space=pl.ANY)] * len(skipped),
        out_specs=[pl.BlockSpec(memory_space=pl.ANY), VMEM],
        out_shape=[jax.ShapeDtypeStruct((deep, wide), F32), jax.ShapeDtypeStruct((8, 128), F32)],
        scratch_shapes=[
            pltpu.VMEM((SLOTS, part, count), F32),
            pltpu.SemaphoreType.DMA((SLOTS,)),
            pltpu.VMEM((len(jobs), 4 * rows, count), BF16),
        ],
        input_output_aliases={} if base is None else {len(ins) - 1: 0},
        compiler_params=params(14),
        cost_estimate=cost(0, 4 * count * sum(job[3] - job[2] for job in jobs)),
        name="weight_part",
    )(*ins)


def pair_kernel(*refs):
    keep_ref, got_ref, outs = refs[0], refs[1], refs[3:]
    for mask in range(len(outs)):
        outs[mask][...] = keep_ref[mask] + got_ref[mask]


def pair_sums(keep, got, after):
    n, size, deep = keep.shape
    return pl.pallas_call(
        pair_kernel,
        in_specs=[VMEM] * 2 + [pl.BlockSpec(memory_space=pl.ANY)],
        out_specs=[VMEM] * n,
        out_shape=[jax.ShapeDtypeStruct((size, deep), F32)] * n,
        compiler_params=params(),
        cost_estimate=cost(0, 12 * n * size * deep),
        name="pair_sums",
    )(keep, got, after)


def add_kernel(*refs):
    total = refs[0][...]
    for ref in refs[1:-1]:
        total = total + ref[...]
    refs[-1][...] = total


def add_up(parts):
    return pl.pallas_call(
        add_kernel,
        in_specs=[VMEM] * len(parts),
        out_specs=VMEM,
        out_shape=jax.ShapeDtypeStruct(parts[0].shape, F32),
        compiler_params=params(),
        name="add_up",
    )(*parts)


def body(inputs, weight, upstream):
    n_mp, n_hid = lax.axis_size("mp"), lax.axis_size("hidden")
    wide = weight.shape[1]
    cut = wide // 2
    ranges = [(0, cut), (cut, wide - cut)]

    held_a = load_weight(weight, 0, cut)
    own = lay_rows([inputs] + [swap(inputs, "hidden", 2 * mask) for mask in range(1, n_hid // 2)], held_a)
    x = order_rows(own, swap(own, "hidden", 1), n_mp, inputs.shape[0])
    part_a, held_b = partial_pre(x, held_a, weight, *ranges[1], n_mp, True)
    part_b, held_c = partial_pre(x, held_b, weight, *ranges[1], n_mp, False)
    turned = turn_rows(x)

    def exchange(own):
        return [own[0]] + [swap(own[mask], "mp", mask) for mask in range(1, n_mp)]

    got_a = exchange(part_a)
    mine_a, _ = grad_mine(got_a, upstream, 0)
    mine_b, _ = grad_mine(exchange(part_b), upstream, cut)
    grad_a, grad_b = [[mine] + [swap(mine, "mp", mask) for mask in range(1, n_mp)] for mine in (mine_a, mine_b)]

    (total,) = input_share([held_a], grad_a, None, n_hid, False)
    keep, send = input_share([held_b, held_c], grad_b, total, n_hid, True)
    deep = turned.shape[0]
    part = fit(deep // 4, 128)
    early = part * max(1, deep // part * EARLY // 16)
    weight_grad, mark = weight_part(turned, [(grad_a, 0, 0, early)], part, None, keep, wide)
    sums = pair_sums(keep, swap(send, "hidden", 1), mark)
    jobs = [(grad_a, 0, early, deep), (grad_b, cut, 0, deep)]
    weight_grad, _ = weight_part(turned, jobs, part, weight_grad, sums[0], wide)
    input_grad = add_up([sums[0]] + [swap(sums[mask], "hidden", 2 * mask) for mask in range(1, n_hid // 2)])
    return input_grad, weight_grad


def solution(mesh):
    placed = (P("hidden", "mp"), P("mp", "hidden"), P("mp", "hidden"))
    return jax.shard_map(
        body,
        mesh=mesh,
        in_specs=placed,
        out_specs=(P("hidden", "mp"), P("mp", "hidden")),
        check_vma=False,
    )
```

time: 93.6 us -> 71.6 us (0.76)
  Pallas kernels: 57.8 us -> 38.9 us
  waiting for transfers between devices: 7.71 us -> 5.13 us
    pallas_call x11 -> x12, Pallas kernels: 56.8 us -> 37.9 us  [the longest x2 13.2 us: weight_part(): pl.pallas_call(functools.partial(weight_kernel, n_mp, part, [job[1:] for...]
    ppermute x20, waiting for transfers between devices: 7.71 us -> 5.13 us  [swap(): return lax.ppermute(value, axis, [(i, i ^ mask) for i in range(size)])]
  transfers between devices with their start and end apart: 20 -> 20, of which waited for: 3 -> 5; matrix products, arithmetic and copies ran while one was open for 0% -> 0% of each run, Pallas kernels for 48% -> 41%
where the time goes in v3:
time: 71.6 us; the launch traced here: 71.4 us
  Pallas kernels  38.9 us (54%)
  starting transfers between devices  26.6 us (37%)
  waiting for transfers between devices  5.13 us (7%)
  between operations  0.83 us (1%)
    ppermute x20, starting transfers between devices, swap(): return lax.ppermute(value, axis, [(i, i ^ mask) for i in range(size)])  26.6 us
    pallas_call x2, Pallas kernels, weight_part(): pl.pallas_call(functools.partial(weight_kernel, n_mp, part, [job[1:] for...  13.2 us
    pallas_call x2, Pallas kernels, input_share(): pl.pallas_call(functools.partial(input_kernel, n_mp, len(weights), block,...  10.4 us
    pallas_call x2, Pallas kernels, partial_pre(): pl.pallas_call(kernel, in_specs=[VMEM, VMEM, pl.BlockSpec(memory_space=pl...  8.07 us
    pallas_call x1, Pallas kernels, load_weight(): pl.pallas_call(functools.partial(load_kernel, first, block), in_specs=[pl...  5.92 us
    ppermute x20, waiting for transfers between devices, swap(): return lax.ppermute(value, axis, [(i, i ^ mask) for i in range(size)])  5.13 us
  transfers between devices with their start and end apart: 20, of which 5 were waited for; matrix products, arithmetic and copies ran while one was open for 0% of the time, Pallas kernels for 41%

profile of v3, /device:TPU:0, one launch (start us, length us, event | category | flops | bytes accessed | tf_op | source)
XLA Modules:
  0.0 71.4 jit_solution(8257300539533179146)
XLA Ops:
  0.6 3.1 %collective-permute-start = (f32[8,2048]{1,0:T(8,128)}, f32[8,2048]{1,0:T(8,128)S(1)}, u32[]{:S(2)}, u32[]{:S(2)}) collective-permute-start(f32[8,2048]{1,0:T(8,128)} %refs_1_.1), channel_id=1, source_target_pairs={{0,2},{1,3},{2,0},{3,1},{4,6},{5,7},{6,4},{7,5},{8,10},{9,11},{10,... | collective-permute-start | bytes 196616 | tf_op jit(solution)/shard_map/ppermute | solution.py:38
  3.7 2.6 %collective-permute-start.1 = (f32[8,2048]{1,0:T(8,128)}, f32[8,2048]{1,0:T(8,128)S(1)}, u32[]{:S(2)}, u32[]{:S(2)}) collective-permute-start(f32[8,2048]{1,0:T(8,128)} %refs_1_.1), channel_id=1, source_target_pairs={{0,4},{1,5},{2,6},{3,7},{4,0},{5,1},{6,2},{7,3},{8,12},{9,13},{10,... | collective-permute-start | bytes 196616 | tf_op jit(solution)/shard_map/ppermute | solution.py:38
  6.3 5.9 %load_weight.1.refs_0_.w_ref = f32[2048,2048]{1,0:T(8,128)S(1)} custom-call(f32[2048,4096]{1,0:T(8,128)} %all_ref.3), custom_call_target="tpu_custom_call" | custom-call | bytes 16777216 | tf_op jit(solution)/shard_map/load_weight/pallas_call | solution.py:61
  12.3 0.3 collective-permute-done.2.refs_4_
  12.7 1.5 %collective-permute-done.3.other_ref = f32[32,2048]{1,0:T(8,128)S(1)} collective-permute-done((f32[32,2048]{1,0:T(8,128)S(1)}, f32[32,2048]{1,0:T(8,128)S(1)}, u32[]{:S(2)}, u32[]{:S(2)}) %collective-permute-start.3) | collective-permute-done | bytes 262176 | tf_op jit(solution)/shard_map/ppermute | solution.py:38
  14.2 0.1 order_rows.1.x_ref
  14.4 3.8 %partial_pre.2 = (f32[16,2048]{1,0:T(8,128)S(1)}, f32[16,2048]{1,0:T(8,128)S(1)}, f32[16,2048]{1,0:T(8,128)S(1)}, f32[16,2048]{1,0:T(8,128)S(1)}, f32[1024,2048]{1,0:T(8,128)S(1)}) custom-call(bf16[128,2048]{1,0:T(8,128)(2,1)S(1)} %order_rows.1.x_ref, f32[2048,2048]{1,0:T(8,128)S(1)} %load_weight.1.refs_0_.w_ref, f32[2048,4096]{1,0:T(8,128)} %all_ref.3), custom_call_target="tpu_custom_call" | custom-call | flops 5368709120 | bytes 524288 | tf_op jit(solution)/shard_map/partial_pre/pallas_call | solution.py:212
  18.2 1.6 %collective-permute-start.10 = (f32[16,2048]{1,0:T(8,128)S(1)}, f32[16,2048]{1,0:T(8,128)S(1)}, u32[]{:S(2)}, u32[]{:S(2)}) collective-permute-start(f32[16,2048]{1,0:T(8,128)S(1)} %get-tuple-element.28), channel_id=1, source_target_pairs={{0,8},{8,0},{16,24},{24,16},{1,9},{9,1},{17,25},{25,17},{2,10},{10... | collective-permute-start | bytes 393224 | tf_op jit(solution)/shard_map/ppermute | solution.py:38
  19.8 1.5 %collective-permute-start.11 = (f32[16,2048]{1,0:T(8,128)S(1)}, f32[16,2048]{1,0:T(8,128)S(1)}, u32[]{:S(2)}, u32[]{:S(2)}) collective-permute-start(f32[16,2048]{1,0:T(8,128)S(1)} %get-tuple-element.29), channel_id=1, source_target_pairs={{0,16},{8,24},{16,0},{24,8},{1,17},{9,25},{17,1},{25,9},{2,18},{10... | collective-permute-start | bytes 393224 | tf_op jit(solution)/shard_map/ppermute | solution.py:38
  21.3 0.5 collective-permute-start.12
  21.8 4.2 %partial_pre.3 = (f32[16,2048]{1,0:T(8,128)S(1)}, f32[16,2048]{1,0:T(8,128)S(1)}, f32[16,2048]{1,0:T(8,128)S(1)}, f32[16,2048]{1,0:T(8,128)S(1)}, f32[1024,2048]{1,0:T(8,128)S(1)}) custom-call(bf16[128,2048]{1,0:T(8,128)(2,1)S(1)} %order_rows.1.x_ref, f32[1024,2048]{1,0:T(8,128)S(1)} %get-tuple-element.21.old_ref.refs_0_, f32[2048,4096]{1,0:T(8,128)} %all_ref.3), custom_call_target="tpu_custom_call" | custom-call | flops 5368709120 | bytes 524288 | tf_op jit(solution)/shard_map/partial_pre/pallas_call | solution.py:212
  26.0 1.6 %collective-permute-start.4 = (f32[16,2048]{1,0:T(8,128)S(1)}, f32[16,2048]{1,0:T(8,128)S(1)}, u32[]{:S(2)}, u32[]{:S(2)}) collective-permute-start(f32[16,2048]{1,0:T(8,128)S(1)} %get-tuple-element.24), channel_id=1, source_target_pairs={{0,8},{8,0},{16,24},{24,16},{1,9},{9,1},{17,25},{25,17},{2,10},{10... | collective-permute-start | bytes 393224 | tf_op jit(solution)/shard_map/ppermute | solution.py:38
  27.6 1.5 %collective-permute-start.5 = (f32[16,2048]{1,0:T(8,128)S(1)}, f32[16,2048]{1,0:T(8,128)S(1)}, u32[]{:S(2)}, u32[]{:S(2)}) collective-permute-start(f32[16,2048]{1,0:T(8,128)S(1)} %get-tuple-element.25), channel_id=1, source_target_pairs={{0,16},{8,24},{16,0},{24,8},{1,17},{9,25},{17,1},{25,9},{2,18},{10... | collective-permute-start | bytes 393224 | tf_op jit(solution)/shard_map/ppermute | solution.py:38
  29.1 0.5 collective-permute-start.6
  29.7 1.6 %collective-permute-start.13 = (f32[16,2048]{1,0:T(8,128)S(1)}, f32[16,2048]{1,0:T(8,128)S(1)}, u32[]{:S(2)}, u32[]{:S(2)}) collective-permute-start(f32[16,2048]{1,0:T(8,128)S(1)} %grad_mine.3.refs_1_.refs_0_), channel_id=1, source_target_pairs={{0,8},{8,0},{16,24},{24,16},{1,9},{9,1},{17,25},{25,17},{2,10},{10... | collective-permute-start | bytes 393224 | tf_op jit(solution)/shard_map/ppermute | solution.py:38
  31.2 1.5 %collective-permute-start.14 = (f32[16,2048]{1,0:T(8,128)S(1)}, f32[16,2048]{1,0:T(8,128)S(1)}, u32[]{:S(2)}, u32[]{:S(2)}) collective-permute-start(f32[16,2048]{1,0:T(8,128)S(1)} %grad_mine.3.refs_1_.refs_0_), channel_id=1, source_target_pairs={{0,16},{8,24},{16,0},{24,8},{1,17},{9,25},{17,1},{25,9},{2,18},{10... | collective-permute-start | bytes 393224 | tf_op jit(solution)/shard_map/ppermute | solution.py:38
  32.8 2.1 %collective-permute-start.15 = (f32[16,2048]{1,0:T(8,128)S(1)}, f32[16,2048]{1,0:T(8,128)S(1)}, u32[]{:S(2)}, u32[]{:S(2)}) collective-permute-start(f32[16,2048]{1,0:T(8,128)S(1)} %grad_mine.3.refs_1_.refs_0_), channel_id=1, source_target_pairs={{0,24},{8,16},{16,8},{24,0},{1,25},{9,17},{17,9},{25,1},{2,26},{10... | collective-permute-start | bytes 393224 | tf_op jit(solution)/shard_map/ppermute | solution.py:38
  34.9 1.6 %collective-permute-done.5.refs_2_ = f32[16,2048]{1,0:T(8,128)S(1)} collective-permute-done((f32[16,2048]{1,0:T(8,128)S(1)}, f32[16,2048]{1,0:T(8,128)S(1)}, u32[]{:S(2)}, u32[]{:S(2)}) %collective-permute-start.5) | collective-permute-done | bytes 131104 | tf_op jit(solution)/shard_map/ppermute | solution.py:38
  36.6 1.4 %collective-permute-start.7 = (f32[16,2048]{1,0:T(8,128)S(1)}, f32[16,2048]{1,0:T(8,128)S(1)}, u32[]{:S(2)}, u32[]{:S(2)}) collective-permute-start(f32[16,2048]{1,0:T(8,128)S(1)} %grad_mine.2.refs_2_.refs_4_), channel_id=1, source_target_pairs={{0,8},{8,0},{16,24},{24,16},{1,9},{9,1},{17,25},{25,17},{2,10},{10... | collective-permute-start | bytes 393224 | tf_op jit(solution)/shard_map/ppermute | solution.py:38
  38.0 0.8 %collective-permute-start.8 = (f32[16,2048]{1,0:T(8,128)S(1)}, f32[16,2048]{1,0:T(8,128)S(1)}, u32[]{:S(2)}, u32[]{:S(2)}) collective-permute-start(f32[16,2048]{1,0:T(8,128)S(1)} %grad_mine.2.refs_2_.refs_4_), channel_id=1, source_target_pairs={{0,16},{8,24},{16,0},{24,8},{1,17},{9,25},{17,1},{25,9},{2,18},{10... | collective-permute-start | bytes 393224 | tf_op jit(solution)/shard_map/ppermute | solution.py:38
  38.8 1.7 %collective-permute-start.9 = (f32[16,2048]{1,0:T(8,128)S(1)}, f32[16,2048]{1,0:T(8,128)S(1)}, u32[]{:S(2)}, u32[]{:S(2)}) collective-permute-start(f32[16,2048]{1,0:T(8,128)S(1)} %grad_mine.2.refs_2_.refs_4_), channel_id=1, source_target_pairs={{0,24},{8,16},{16,8},{24,0},{1,25},{9,17},{17,9},{25,1},{2,26},{10... | collective-permute-start | bytes 393224 | tf_op jit(solution)/shard_map/ppermute | solution.py:38
  40.5 1.2 %collective-permute-done.14.refs_3_.refs_2_ = f32[16,2048]{1,0:T(8,128)S(1)} collective-permute-done((f32[16,2048]{1,0:T(8,128)S(1)}, f32[16,2048]{1,0:T(8,128)S(1)}, u32[]{:S(2)}, u32[]{:S(2)}) %collective-permute-start.14) | collective-permute-done | bytes 131104 | tf_op jit(solution)/shard_map/ppermute | solution.py:38
  41.7 0.5 collective-permute-done.15.refs_4_.refs_3_
  42.2 5.4 %input_share.2.refs_6_ = f32[64,2048]{1,0:T(8,128)S(1)} custom-call(f32[2048,2048]{1,0:T(8,128)S(1)} %load_weight.1.refs_0_.w_ref, f32[16,2048]{1,0:T(8,128)S(1)} %grad_mine.3.refs_1_.refs_0_, f32[16,2048]{1,0:T(8,128)S(1)} %collective-permute-done.13.refs_2_.refs_1_, f32[16,2048]{1,0:T(8,128)S(1)} %collective-permute-done.14.refs_3_.refs_2_, ...), custom_call_target="tpu_custom_call" | custom-call | flops 5368709120 | bytes 524288 | tf_op jit(solution)/shard_map/input_share/pallas_call | solution.py:304
  47.6 5.0 %input_share.3 = (f32[4,8,2048]{2,1,0:T(8,128)S(1)}, f32[4,8,2048]{2,1,0:T(8,128)S(1)}) custom-call(f32[1024,2048]{1,0:T(8,128)S(1)} %get-tuple-element.21.old_ref.refs_0_, f32[1024,2048]{1,0:T(8,128)S(1)} %get-tuple-element.22.refs_1_, f32[16,2048]{1,0:T(8,128)S(1)} %grad_mine.2.refs_2_.refs_4_, f32[16,2048]{1,0:T(8,128)S(1)} %collective-permute-done.7.refs_3_.refs_5_, ...), custom_call_target="tpu_custom_call" | custom-call | flops 5368709120 | bytes 524288 | tf_op jit(solution)/shard_map/input_share/pallas_call | solution.py:304
  52.7 0.3 turn_rows.1.t_ref
  53.0 2.5 %weight_part.2 = (f32[2048,4096]{1,0:T(8,128)}, f32[8,128]{1,0:T(8,128)S(1)}) custom-call(bf16[2048,256]{1,0:T(8,128)(2,1)S(1)} %turn_rows.1.t_ref, f32[16,2048]{1,0:T(8,128)S(1)} %grad_mine.3.refs_1_.refs_0_, f32[16,2048]{1,0:T(8,128)S(1)} %collective-permute-done.13.refs_2_.refs_1_, f32[16,2048]{1,0:T(8,128)S(1)} %collective-permute-done.14.refs_3_.refs_2_, ...), custom_call_target="tpu_custom_call" | custom-call | bytes 4194304 | tf_op jit(solution)/shard_map/weight_part/pallas_call | solution.py:357
  55.6 0.7 collective-permute-start.17
  56.3 3.4 %collective-permute-start.18 = (f32[8,2048]{1,0:T(8,128)S(1)}, f32[8,2048]{1,0:T(8,128)S(1)}, u32[]{:S(2)}, u32[]{:S(2)}) collective-permute-start(f32[8,2048]{1,0:T(8,128)S(1)} %get-tuple-element.36), channel_id=1, source_target_pairs={{0,4},{1,5},{2,6},{3,7},{4,0},{5,1},{6,2},{7,3},{8,12},{9,13},{10,... | collective-permute-start | bytes 196616 | tf_op jit(solution)/shard_map/ppermute | solution.py:38
  59.7 0.3 collective-permute-start.19
  60.0 10.7 %weight_part.3 = (f32[2048,4096]{1,0:T(8,128)}, f32[8,128]{1,0:T(8,128)}) custom-call(bf16[2048,256]{1,0:T(8,128)(2,1)S(1)} %turn_rows.1.t_ref, f32[16,2048]{1,0:T(8,128)S(1)} %grad_mine.3.refs_1_.refs_0_, f32[16,2048]{1,0:T(8,128)S(1)} %collective-permute-done.13.refs_2_.refs_1_, ...), custom_call_target="tpu_custom_call", output_to_operand_aliasing={{0}: (10, {})} | custom-call | bytes 29360128 | tf_op jit(solution)/shard_map/weight_part/pallas_call | solution.py:357
  70.8 0.6 add_up.1
  (26 shorter events, 0.4 us)
Async XLA Ops:
  0.6 12.0 %copy-start.1 = (f32[8,2048]{1,0:T(8,128)S(1)}, f32[8,2048]{1,0:T(8,128)}, u32[]{:S(2)}) copy-start(f32[8,2048]{1,0:T(8,128)} %refs_1_.1) | copy-start | bytes 196612
  0.6 11.6 %collective-permute-start = (f32[8,2048]{1,0:T(8,128)}, f32[8,2048]{1,0:T(8,128)S(1)}, u32[]{:S(2)}, u32[]{:S(2)}) collective-permute-start(f32[8,2048]{1,0:T(8,128)} %refs_1_.1), channel_id=1, source_target_pairs={{0,2},{1,3},{2,0},{3,1},{4,6},{5,7},{6,4},{7,5},{8,10},{9,11},{10,... | collective-permute-start | bytes 196616 | tf_op jit(solution)/shard_map/ppermute | solution.py:38
  3.7 8.5 %collective-permute-start.1 = (f32[8,2048]{1,0:T(8,128)}, f32[8,2048]{1,0:T(8,128)S(1)}, u32[]{:S(2)}, u32[]{:S(2)}) collective-permute-start(f32[8,2048]{1,0:T(8,128)} %refs_1_.1), channel_id=1, source_target_pairs={{0,4},{1,5},{2,6},{3,7},{4,0},{5,1},{6,2},{7,3},{8,12},{9,13},{10,... | collective-permute-start | bytes 196616 | tf_op jit(solution)/shard_map/ppermute | solution.py:38
  6.3 6.3 %collective-permute-start.2 = (f32[8,2048]{1,0:T(8,128)}, f32[8,2048]{1,0:T(8,128)S(1)}, u32[]{:S(2)}, u32[]{:S(2)}) collective-permute-start(f32[8,2048]{1,0:T(8,128)} %refs_1_.1), channel_id=1, source_target_pairs={{0,6},{1,7},{2,4},{3,5},{4,2},{5,3},{6,0},{7,1},{8,14},{9,15},{10,... | collective-permute-start | bytes 196616 | tf_op jit(solution)/shard_map/ppermute | solution.py:38
  12.6 1.6 %collective-permute-start.3 = (f32[32,2048]{1,0:T(8,128)S(1)}, f32[32,2048]{1,0:T(8,128)S(1)}, u32[]{:S(2)}, u32[]{:S(2)}) collective-permute-start(f32[32,2048]{1,0:T(8,128)S(1)} %lay_rows.1.own_ref), channel_id=1, source_target_pairs={{0,1},{1,0},{2,3},{3,2},{4,5},{5,4},{6,7},{7,6},{8,9},{9,8},{10,11... | collective-permute-start | bytes 786440 | tf_op jit(solution)/shard_map/ppermute | solution.py:38
  18.2 11.4 %copy-start = (f32[16,4096]{1,0:T(8,128)S(1)}, f32[16,4096]{1,0:T(8,128)}, u32[]{:S(2)}) copy-start(f32[16,4096]{1,0:T(8,128)} %refs_4_.3) | copy-start | bytes 786436
  18.2 10.9 %collective-permute-start.10 = (f32[16,2048]{1,0:T(8,128)S(1)}, f32[16,2048]{1,0:T(8,128)S(1)}, u32[]{:S(2)}, u32[]{:S(2)}) collective-permute-start(f32[16,2048]{1,0:T(8,128)S(1)} %get-tuple-element.28), channel_id=1, source_target_pairs={{0,8},{8,0},{16,24},{24,16},{1,9},{9,1},{17,25},{25,17},{2,10},{10... | collective-permute-start | bytes 393224 | tf_op jit(solution)/shard_map/ppermute | solution.py:38
  19.8 9.8 %collective-permute-start.11 = (f32[16,2048]{1,0:T(8,128)S(1)}, f32[16,2048]{1,0:T(8,128)S(1)}, u32[]{:S(2)}, u32[]{:S(2)}) collective-permute-start(f32[16,2048]{1,0:T(8,128)S(1)} %get-tuple-element.29), channel_id=1, source_target_pairs={{0,16},{8,24},{16,0},{24,8},{1,17},{9,25},{17,1},{25,9},{2,18},{10... | collective-permute-start | bytes 393224 | tf_op jit(solution)/shard_map/ppermute | solution.py:38
  21.3 8.3 %collective-permute-start.12 = (f32[16,2048]{1,0:T(8,128)S(1)}, f32[16,2048]{1,0:T(8,128)S(1)}, u32[]{:S(2)}, u32[]{:S(2)}) collective-permute-start(f32[16,2048]{1,0:T(8,128)S(1)} %get-tuple-element.30), channel_id=1, source_target_pairs={{0,24},{8,16},{16,8},{24,0},{1,25},{9,17},{17,9},{25,1},{2,26},{10... | collective-permute-start | bytes 393224 | tf_op jit(solution)/shard_map/ppermute | solution.py:38
  26.0 6.7 %collective-permute-start.4 = (f32[16,2048]{1,0:T(8,128)S(1)}, f32[16,2048]{1,0:T(8,128)S(1)}, u32[]{:S(2)}, u32[]{:S(2)}) collective-permute-start(f32[16,2048]{1,0:T(8,128)S(1)} %get-tuple-element.24), channel_id=1, source_target_pairs={{0,8},{8,0},{16,24},{24,16},{1,9},{9,1},{17,25},{25,17},{2,10},{10... | collective-permute-start | bytes 393224 | tf_op jit(solution)/shard_map/ppermute | solution.py:38
  27.6 8.9 %collective-permute-start.5 = (f32[16,2048]{1,0:T(8,128)S(1)}, f32[16,2048]{1,0:T(8,128)S(1)}, u32[]{:S(2)}, u32[]{:S(2)}) collective-permute-start(f32[16,2048]{1,0:T(8,128)S(1)} %get-tuple-element.25), channel_id=1, source_target_pairs={{0,16},{8,24},{16,0},{24,8},{1,17},{9,25},{17,1},{25,9},{2,18},{10... | collective-permute-start | bytes 393224 | tf_op jit(solution)/shard_map/ppermute | solution.py:38
  29.1 7.4 %collective-permute-start.6 = (f32[16,2048]{1,0:T(8,128)S(1)}, f32[16,2048]{1,0:T(8,128)S(1)}, u32[]{:S(2)}, u32[]{:S(2)}) collective-permute-start(f32[16,2048]{1,0:T(8,128)S(1)} %get-tuple-element.26), channel_id=1, source_target_pairs={{0,24},{8,16},{16,8},{24,0},{1,25},{9,17},{17,9},{25,1},{2,26},{10... | collective-permute-start | bytes 393224 | tf_op jit(solution)/shard_map/ppermute | solution.py:38
  29.7 9.1 %collective-permute-start.13 = (f32[16,2048]{1,0:T(8,128)S(1)}, f32[16,2048]{1,0:T(8,128)S(1)}, u32[]{:S(2)}, u32[]{:S(2)}) collective-permute-start(f32[16,2048]{1,0:T(8,128)S(1)} %grad_mine.3.refs_1_.refs_0_), channel_id=1, source_target_pairs={{0,8},{8,0},{16,24},{24,16},{1,9},{9,1},{17,25},{25,17},{2,10},{10... | collective-permute-start | bytes 393224 | tf_op jit(solution)/shard_map/ppermute | solution.py:38
  31.2 10.4 %collective-permute-start.14 = (f32[16,2048]{1,0:T(8,128)S(1)}, f32[16,2048]{1,0:T(8,128)S(1)}, u32[]{:S(2)}, u32[]{:S(2)}) collective-permute-start(f32[16,2048]{1,0:T(8,128)S(1)} %grad_mine.3.refs_1_.refs_0_), channel_id=1, source_target_pairs={{0,16},{8,24},{16,0},{24,8},{1,17},{9,25},{17,1},{25,9},{2,18},{10... | collective-permute-start | bytes 393224 | tf_op jit(solution)/shard_map/ppermute | solution.py:38
  32.8 9.4 %collective-permute-start.15 = (f32[16,2048]{1,0:T(8,128)S(1)}, f32[16,2048]{1,0:T(8,128)S(1)}, u32[]{:S(2)}, u32[]{:S(2)}) collective-permute-start(f32[16,2048]{1,0:T(8,128)S(1)} %grad_mine.3.refs_1_.refs_0_), channel_id=1, source_target_pairs={{0,24},{8,16},{16,8},{24,0},{1,25},{9,17},{17,9},{25,1},{2,26},{10... | collective-permute-start | bytes 393224 | tf_op jit(solution)/shard_map/ppermute | solution.py:38
  36.6 11.0 %collective-permute-start.7 = (f32[16,2048]{1,0:T(8,128)S(1)}, f32[16,2048]{1,0:T(8,128)S(1)}, u32[]{:S(2)}, u32[]{:S(2)}) collective-permute-start(f32[16,2048]{1,0:T(8,128)S(1)} %grad_mine.2.refs_2_.refs_4_), channel_id=1, source_target_pairs={{0,8},{8,0},{16,24},{24,16},{1,9},{9,1},{17,25},{25,17},{2,10},{10... | collective-permute-start | bytes 393224 | tf_op jit(solution)/shard_map/ppermute | solution.py:38
  38.0 9.6 %collective-permute-start.8 = (f32[16,2048]{1,0:T(8,128)S(1)}, f32[16,2048]{1,0:T(8,128)S(1)}, u32[]{:S(2)}, u32[]{:S(2)}) collective-permute-start(f32[16,2048]{1,0:T(8,128)S(1)} %grad_mine.2.refs_2_.refs_4_), channel_id=1, source_target_pairs={{0,16},{8,24},{16,0},{24,8},{1,17},{9,25},{17,1},{25,9},{2,18},{10... | collective-permute-start | bytes 393224 | tf_op jit(solution)/shard_map/ppermute | solution.py:38
  38.8 8.8 %collective-permute-start.9 = (f32[16,2048]{1,0:T(8,128)S(1)}, f32[16,2048]{1,0:T(8,128)S(1)}, u32[]{:S(2)}, u32[]{:S(2)}) collective-permute-start(f32[16,2048]{1,0:T(8,128)S(1)} %grad_mine.2.refs_2_.refs_4_), channel_id=1, source_target_pairs={{0,24},{8,16},{16,8},{24,0},{1,25},{9,17},{17,9},{25,1},{2,26},{10... | collective-permute-start | bytes 393224 | tf_op jit(solution)/shard_map/ppermute | solution.py:38
  52.6 2.9 %collective-permute-start.16 = (f32[4,8,2048]{2,1,0:T(8,128)S(1)}, f32[4,8,2048]{2,1,0:T(8,128)S(1)}, u32[]{:S(2)}, u32[]{:S(2)}) collective-permute-start(f32[4,8,2048]{2,1,0:T(8,128)S(1)} %get-tuple-element.32), channel_id=1, source_target_pairs={{0,1},{1,0},{2,3},{3,2},{4,5},{5,4},{6,7},{7,6},{8,9},{9,8},{10,11... | collective-permute-start | bytes 786440 | tf_op jit(solution)/shard_map/ppermute | solution.py:38
  55.6 15.2 %collective-permute-start.17 = (f32[8,2048]{1,0:T(8,128)S(1)}, f32[8,2048]{1,0:T(8,128)S(1)}, u32[]{:S(2)}, u32[]{:S(2)}) collective-permute-start(f32[8,2048]{1,0:T(8,128)S(1)} %get-tuple-element.35), channel_id=1, source_target_pairs={{0,2},{1,3},{2,0},{3,1},{4,6},{5,7},{6,4},{7,5},{8,10},{9,11},{10,... | collective-permute-start | bytes 196616 | tf_op jit(solution)/shard_map/ppermute | solution.py:38
  56.3 14.5 %collective-permute-start.18 = (f32[8,2048]{1,0:T(8,128)S(1)}, f32[8,2048]{1,0:T(8,128)S(1)}, u32[]{:S(2)}, u32[]{:S(2)}) collective-permute-start(f32[8,2048]{1,0:T(8,128)S(1)} %get-tuple-element.36), channel_id=1, source_target_pairs={{0,4},{1,5},{2,6},{3,7},{4,0},{5,1},{6,2},{7,3},{8,12},{9,13},{10,... | collective-permute-start | bytes 196616 | tf_op jit(solution)/shard_map/ppermute | solution.py:38
  59.7 11.1 %collective-permute-start.19 = (f32[8,2048]{1,0:T(8,128)S(1)}, f32[8,2048]{1,0:T(8,128)S(1)}, u32[]{:S(2)}, u32[]{:S(2)}) collective-permute-start(f32[8,2048]{1,0:T(8,128)S(1)} %get-tuple-element.37), channel_id=1, source_target_pairs={{0,6},{1,7},{2,4},{3,5},{4,2},{5,3},{6,0},{7,1},{8,14},{9,15},{10,... | collective-permute-start | bytes 196616 | tf_op jit(solution)/shard_map/ppermute | solution.py:38

commit v4 on v3

--- a/solution.py
+++ b/solution.py
@@ -81,7 +81,7 @@
 def lay_kernel(*refs):
     refs = refs[1:]
     size = refs[0].shape[0]
-    for mask, ref in enumerate(refs[:-1]):
+    for mask, ref in enumerate(reversed(refs[:-1])):
         refs[-1][mask * size : (mask + 1) * size, :] = ref[...]
 
 
@@ -415,7 +415,7 @@
     ranges = [(0, cut), (cut, wide - cut)]
 
     held_a = load_weight(weight, 0, cut)
-    own = lay_rows([inputs] + [swap(inputs, "hidden", 2 * mask) for mask in range(1, n_hid // 2)], held_a)
+    own = lay_rows([swap(inputs, "hidden", 2 * mask) for mask in range(n_hid // 2 - 1, 0, -1)] + [inputs], held_a)
     x = order_rows(own, swap(own, "hidden", 1), n_mp, inputs.shape[0])
     part_a, held_b = partial_pre(x, held_a, weight, *ranges[1], n_mp, True)
     part_b, held_c = partial_pre(x, held_b, weight, *ranges[1], n_mp, False)
@@ -438,7 +438,7 @@
     sums = pair_sums(keep, swap(send, "hidden", 1), mark)
     jobs = [(grad_a, 0, early, deep), (grad_b, cut, 0, deep)]
     weight_grad, _ = weight_part(turned, jobs, part, weight_grad, sums[0], wide)
-    input_grad = add_up([sums[0]] + [swap(sums[mask], "hidden", 2 * mask) for mask in range(1, n_hid // 2)])
+    input_grad = add_up([swap(sums[mask], "hidden", 2 * mask) for mask in range(n_hid // 2 - 1, 0, -1)] + [sums[0]])
     return input_grad, weight_grad
 
 

time: 71.6 us -> 71.5 us (level)
  transfers between devices with their start and end apart: 20 -> 20, of which waited for: 5 -> 4; matrix products, arithmetic and copies ran while one was open for 0% -> 0% of each run, Pallas kernels for 41% -> 41%
where the time goes in v4:
time: 71.5 us; the launch traced here: 71.3 us
  Pallas kernels  38.9 us (54%)
  starting transfers between devices  26.8 us (37%)
  waiting for transfers between devices  4.75 us (7%)
  between operations  0.85 us (1%)
    ppermute x20, starting transfers between devices, swap(): return lax.ppermute(value, axis, [(i, i ^ mask) for i in range(size)])  26.8 us
    pallas_call x2, Pallas kernels, weight_part(): pl.pallas_call(functools.partial(weight_kernel, n_mp, part, [job[1:] for...  13.2 us
    pallas_call x2, Pallas kernels, input_share(): pl.pallas_call(functools.partial(input_kernel, n_mp, len(weights), block,...  10.4 us
    pallas_call x2, Pallas kernels, partial_pre(): pl.pallas_call(kernel, in_specs=[VMEM, VMEM, pl.BlockSpec(memory_space=pl...  8.08 us
    pallas_call x1, Pallas kernels, load_weight(): pl.pallas_call(functools.partial(load_kernel, first, block), in_specs=[pl...  5.92 us
    ppermute x20, waiting for transfers between devices, swap(): return lax.ppermute(value, axis, [(i, i ^ mask) for i in range(size)])  4.75 us
  transfers between devices with their start and end apart: 20, of which 4 were waited for; matrix products, arithmetic and copies ran while one was open for 0% of the time, Pallas kernels for 41%

profile of v4, /device:TPU:0, one launch (start us, length us, event | category | flops | bytes accessed | tf_op | source)
XLA Modules:
  0.0 71.3 jit_solution(16970126850788927039)
XLA Ops:
  0.6 5.1 %collective-permute-start = (f32[8,2048]{1,0:T(8,128)}, f32[8,2048]{1,0:T(8,128)S(1)}, u32[]{:S(2)}, u32[]{:S(2)}) collective-permute-start(f32[8,2048]{1,0:T(8,128)} %refs_4_.3), channel_id=1, source_target_pairs={{0,6},{1,7},{2,4},{3,5},{4,2},{5,3},{6,0},{7,1},{8,14},{9,15},{10,... | collective-permute-start | bytes 196616 | tf_op jit(solution)/shard_map/ppermute | solution.py:38
  5.8 0.6 collective-permute-start.2
  6.4 5.9 %load_weight.1.refs_0_.w_ref = f32[2048,2048]{1,0:T(8,128)S(1)} custom-call(f32[2048,4096]{1,0:T(8,128)} %all_ref.3), custom_call_target="tpu_custom_call" | custom-call | bytes 16777216 | tf_op jit(solution)/shard_map/load_weight/pallas_call | solution.py:61
  12.5 1.5 %collective-permute-done.3.other_ref = f32[32,2048]{1,0:T(8,128)S(1)} collective-permute-done((f32[32,2048]{1,0:T(8,128)S(1)}, f32[32,2048]{1,0:T(8,128)S(1)}, u32[]{:S(2)}, u32[]{:S(2)}) %collective-permute-start.3) | collective-permute-done | bytes 262176 | tf_op jit(solution)/shard_map/ppermute | solution.py:38
  14.0 0.1 order_rows.1.x_ref
  14.1 3.8 %partial_pre.2 = (f32[16,2048]{1,0:T(8,128)S(1)}, f32[16,2048]{1,0:T(8,128)S(1)}, f32[16,2048]{1,0:T(8,128)S(1)}, f32[16,2048]{1,0:T(8,128)S(1)}, f32[1024,2048]{1,0:T(8,128)S(1)}) custom-call(bf16[128,2048]{1,0:T(8,128)(2,1)S(1)} %order_rows.1.x_ref, f32[2048,2048]{1,0:T(8,128)S(1)} %load_weight.1.refs_0_.w_ref, f32[2048,4096]{1,0:T(8,128)} %all_ref.3), custom_call_target="tpu_custom_call" | custom-call | flops 5368709120 | bytes 524288 | tf_op jit(solution)/shard_map/partial_pre/pallas_call | solution.py:212
  18.0 1.7 %collective-permute-start.10 = (f32[16,2048]{1,0:T(8,128)S(1)}, f32[16,2048]{1,0:T(8,128)S(1)}, u32[]{:S(2)}, u32[]{:S(2)}) collective-permute-start(f32[16,2048]{1,0:T(8,128)S(1)} %get-tuple-element.28), channel_id=1, source_target_pairs={{0,8},{8,0},{16,24},{24,16},{1,9},{9,1},{17,25},{25,17},{2,10},{10... | collective-permute-start | bytes 393224 | tf_op jit(solution)/shard_map/ppermute | solution.py:38
  19.7 1.5 %collective-permute-start.11 = (f32[16,2048]{1,0:T(8,128)S(1)}, f32[16,2048]{1,0:T(8,128)S(1)}, u32[]{:S(2)}, u32[]{:S(2)}) collective-permute-start(f32[16,2048]{1,0:T(8,128)S(1)} %get-tuple-element.29), channel_id=1, source_target_pairs={{0,16},{8,24},{16,0},{24,8},{1,17},{9,25},{17,1},{25,9},{2,18},{10... | collective-permute-start | bytes 393224 | tf_op jit(solution)/shard_map/ppermute | solution.py:38
  21.2 0.3 collective-permute-start.12
  21.5 4.2 %partial_pre.3 = (f32[16,2048]{1,0:T(8,128)S(1)}, f32[16,2048]{1,0:T(8,128)S(1)}, f32[16,2048]{1,0:T(8,128)S(1)}, f32[16,2048]{1,0:T(8,128)S(1)}, f32[1024,2048]{1,0:T(8,128)S(1)}) custom-call(bf16[128,2048]{1,0:T(8,128)(2,1)S(1)} %order_rows.1.x_ref, f32[1024,2048]{1,0:T(8,128)S(1)} %get-tuple-element.21.old_ref.refs_0_, f32[2048,4096]{1,0:T(8,128)} %all_ref.3), custom_call_target="tpu_custom_call" | custom-call | flops 5368709120 | bytes 524288 | tf_op jit(solution)/shard_map/partial_pre/pallas_call | solution.py:212
  25.8 1.7 %collective-permute-start.4 = (f32[16,2048]{1,0:T(8,128)S(1)}, f32[16,2048]{1,0:T(8,128)S(1)}, u32[]{:S(2)}, u32[]{:S(2)}) collective-permute-start(f32[16,2048]{1,0:T(8,128)S(1)} %get-tuple-element.24), channel_id=1, source_target_pairs={{0,8},{8,0},{16,24},{24,16},{1,9},{9,1},{17,25},{25,17},{2,10},{10... | collective-permute-start | bytes 393224 | tf_op jit(solution)/shard_map/ppermute | solution.py:38
  27.5 1.5 %collective-permute-start.5 = (f32[16,2048]{1,0:T(8,128)S(1)}, f32[16,2048]{1,0:T(8,128)S(1)}, u32[]{:S(2)}, u32[]{:S(2)}) collective-permute-start(f32[16,2048]{1,0:T(8,128)S(1)} %get-tuple-element.25), channel_id=1, source_target_pairs={{0,16},{8,24},{16,0},{24,8},{1,17},{9,25},{17,1},{25,9},{2,18},{10... | collective-permute-start | bytes 393224 | tf_op jit(solution)/shard_map/ppermute | solution.py:38
  29.0 0.3 collective-permute-start.6
  29.4 0.1 grad_mine.3.refs_1_.refs_0_
  29.4 1.7 %collective-permute-start.13 = (f32[16,2048]{1,0:T(8,128)S(1)}, f32[16,2048]{1,0:T(8,128)S(1)}, u32[]{:S(2)}, u32[]{:S(2)}) collective-permute-start(f32[16,2048]{1,0:T(8,128)S(1)} %grad_mine.3.refs_1_.refs_0_), channel_id=1, source_target_pairs={{0,8},{8,0},{16,24},{24,16},{1,9},{9,1},{17,25},{25,17},{2,10},{10... | collective-permute-start | bytes 393224 | tf_op jit(solution)/shard_map/ppermute | solution.py:38
  31.1 1.5 %collective-permute-start.14 = (f32[16,2048]{1,0:T(8,128)S(1)}, f32[16,2048]{1,0:T(8,128)S(1)}, u32[]{:S(2)}, u32[]{:S(2)}) collective-permute-start(f32[16,2048]{1,0:T(8,128)S(1)} %grad_mine.3.refs_1_.refs_0_), channel_id=1, source_target_pairs={{0,16},{8,24},{16,0},{24,8},{1,17},{9,25},{17,1},{25,9},{2,18},{10... | collective-permute-start | bytes 393224 | tf_op jit(solution)/shard_map/ppermute | solution.py:38
  32.7 2.1 %collective-permute-start.15 = (f32[16,2048]{1,0:T(8,128)S(1)}, f32[16,2048]{1,0:T(8,128)S(1)}, u32[]{:S(2)}, u32[]{:S(2)}) collective-permute-start(f32[16,2048]{1,0:T(8,128)S(1)} %grad_mine.3.refs_1_.refs_0_), channel_id=1, source_target_pairs={{0,24},{8,16},{16,8},{24,0},{1,25},{9,17},{17,9},{25,1},{2,26},{10... | collective-permute-start | bytes 393224 | tf_op jit(solution)/shard_map/ppermute | solution.py:38
  34.8 1.7 %collective-permute-done.5.refs_2_ = f32[16,2048]{1,0:T(8,128)S(1)} collective-permute-done((f32[16,2048]{1,0:T(8,128)S(1)}, f32[16,2048]{1,0:T(8,128)S(1)}, u32[]{:S(2)}, u32[]{:S(2)}) %collective-permute-start.5) | collective-permute-done | bytes 131104 | tf_op jit(solution)/shard_map/ppermute | solution.py:38
  36.5 0.1 grad_mine.2.refs_2_.refs_4_
  36.6 1.3 %collective-permute-start.7 = (f32[16,2048]{1,0:T(8,128)S(1)}, f32[16,2048]{1,0:T(8,128)S(1)}, u32[]{:S(2)}, u32[]{:S(2)}) collective-permute-start(f32[16,2048]{1,0:T(8,128)S(1)} %grad_mine.2.refs_2_.refs_4_), channel_id=1, source_target_pairs={{0,8},{8,0},{16,24},{24,16},{1,9},{9,1},{17,25},{25,17},{2,10},{10... | collective-permute-start | bytes 393224 | tf_op jit(solution)/shard_map/ppermute | solution.py:38
  37.9 1.3 %collective-permute-start.8 = (f32[16,2048]{1,0:T(8,128)S(1)}, f32[16,2048]{1,0:T(8,128)S(1)}, u32[]{:S(2)}, u32[]{:S(2)}) collective-permute-start(f32[16,2048]{1,0:T(8,128)S(1)} %grad_mine.2.refs_2_.refs_4_), channel_id=1, source_target_pairs={{0,16},{8,24},{16,0},{24,8},{1,17},{9,25},{17,1},{25,9},{2,18},{10... | collective-permute-start | bytes 393224 | tf_op jit(solution)/shard_map/ppermute | solution.py:38
  39.2 1.4 %collective-permute-start.9 = (f32[16,2048]{1,0:T(8,128)S(1)}, f32[16,2048]{1,0:T(8,128)S(1)}, u32[]{:S(2)}, u32[]{:S(2)}) collective-permute-start(f32[16,2048]{1,0:T(8,128)S(1)} %grad_mine.2.refs_2_.refs_4_), channel_id=1, source_target_pairs={{0,24},{8,16},{16,8},{24,0},{1,25},{9,17},{17,9},{25,1},{2,26},{10... | collective-permute-start | bytes 393224 | tf_op jit(solution)/shard_map/ppermute | solution.py:38
  40.6 1.0 %collective-permute-done.14.refs_3_.refs_2_ = f32[16,2048]{1,0:T(8,128)S(1)} collective-permute-done((f32[16,2048]{1,0:T(8,128)S(1)}, f32[16,2048]{1,0:T(8,128)S(1)}, u32[]{:S(2)}, u32[]{:S(2)}) %collective-permute-start.14) | collective-permute-done | bytes 131104 | tf_op jit(solution)/shard_map/ppermute | solution.py:38
  41.6 0.4 collective-permute-done.15.refs_4_.refs_3_
  42.1 5.4 %input_share.2.refs_6_ = f32[64,2048]{1,0:T(8,128)S(1)} custom-call(f32[2048,2048]{1,0:T(8,128)S(1)} %load_weight.1.refs_0_.w_ref, f32[16,2048]{1,0:T(8,128)S(1)} %grad_mine.3.refs_1_.refs_0_, f32[16,2048]{1,0:T(8,128)S(1)} %collective-permute-done.13.refs_2_.refs_1_, f32[16,2048]{1,0:T(8,128)S(1)} %collective-permute-done.14.refs_3_.refs_2_, ...), custom_call_target="tpu_custom_call" | custom-call | flops 5368709120 | bytes 524288 | tf_op jit(solution)/shard_map/input_share/pallas_call | solution.py:304
  47.5 5.0 %input_share.3 = (f32[4,8,2048]{2,1,0:T(8,128)S(1)}, f32[4,8,2048]{2,1,0:T(8,128)S(1)}) custom-call(f32[1024,2048]{1,0:T(8,128)S(1)} %get-tuple-element.21.old_ref.refs_0_, f32[1024,2048]{1,0:T(8,128)S(1)} %get-tuple-element.22.refs_1_, f32[16,2048]{1,0:T(8,128)S(1)} %grad_mine.2.refs_2_.refs_4_, f32[16,2048]{1,0:T(8,128)S(1)} %collective-permute-done.7.refs_3_.refs_5_, ...), custom_call_target="tpu_custom_call" | custom-call | flops 5368709120 | bytes 524288 | tf_op jit(solution)/shard_map/input_share/pallas_call | solution.py:304
  52.6 0.3 turn_rows.1.t_ref
  52.9 2.5 %weight_part.2 = (f32[2048,4096]{1,0:T(8,128)}, f32[8,128]{1,0:T(8,128)S(1)}) custom-call(bf16[2048,256]{1,0:T(8,128)(2,1)S(1)} %turn_rows.1.t_ref, f32[16,2048]{1,0:T(8,128)S(1)} %grad_mine.3.refs_1_.refs_0_, f32[16,2048]{1,0:T(8,128)S(1)} %collective-permute-done.13.refs_2_.refs_1_, f32[16,2048]{1,0:T(8,128)S(1)} %collective-permute-done.14.refs_3_.refs_2_, ...), custom_call_target="tpu_custom_call" | custom-call | bytes 4194304 | tf_op jit(solution)/shard_map/weight_part/pallas_call | solution.py:357
  55.5 3.7 %collective-permute-start.17 = (f32[8,2048]{1,0:T(8,128)S(1)}, f32[8,2048]{1,0:T(8,128)S(1)}, u32[]{:S(2)}, u32[]{:S(2)}) collective-permute-start(f32[8,2048]{1,0:T(8,128)S(1)} %get-tuple-element.34), channel_id=1, source_target_pairs={{0,6},{1,7},{2,4},{3,5},{4,2},{5,3},{6,0},{7,1},{8,14},{9,15},{10,... | collective-permute-start | bytes 196616 | tf_op jit(solution)/shard_map/ppermute | solution.py:38
  59.2 0.8 %collective-permute-start.19 = (f32[8,2048]{1,0:T(8,128)S(1)}, f32[8,2048]{1,0:T(8,128)S(1)}, u32[]{:S(2)}, u32[]{:S(2)}) collective-permute-start(f32[8,2048]{1,0:T(8,128)S(1)} %get-tuple-element.36), channel_id=1, source_target_pairs={{0,2},{1,3},{2,0},{3,1},{4,6},{5,7},{6,4},{7,5},{8,10},{9,11},{10,... | collective-permute-start | bytes 196616 | tf_op jit(solution)/shard_map/ppermute | solution.py:38
  60.0 10.7 %weight_part.3 = (f32[2048,4096]{1,0:T(8,128)}, f32[8,128]{1,0:T(8,128)}) custom-call(bf16[2048,256]{1,0:T(8,128)(2,1)S(1)} %turn_rows.1.t_ref, f32[16,2048]{1,0:T(8,128)S(1)} %grad_mine.3.refs_1_.refs_0_, f32[16,2048]{1,0:T(8,128)S(1)} %collective-permute-done.13.refs_2_.refs_1_, ...), custom_call_target="tpu_custom_call", output_to_operand_aliasing={{0}: (10, {})} | custom-call | bytes 29360128 | tf_op jit(solution)/shard_map/weight_part/pallas_call | solution.py:357
  70.7 0.6 add_up.1
  (26 shorter events, 0.3 us)
Async XLA Ops:
  0.6 11.7 %copy-start.1 = (f32[8,2048]{1,0:T(8,128)S(1)}, f32[8,2048]{1,0:T(8,128)}, u32[]{:S(2)}) copy-start(f32[8,2048]{1,0:T(8,128)} %refs_4_.3) | copy-start | bytes 196612
  0.6 11.7 %collective-permute-start = (f32[8,2048]{1,0:T(8,128)}, f32[8,2048]{1,0:T(8,128)S(1)}, u32[]{:S(2)}, u32[]{:S(2)}) collective-permute-start(f32[8,2048]{1,0:T(8,128)} %refs_4_.3), channel_id=1, source_target_pairs={{0,6},{1,7},{2,4},{3,5},{4,2},{5,3},{6,0},{7,1},{8,14},{9,15},{10,... | collective-permute-start | bytes 196616 | tf_op jit(solution)/shard_map/ppermute | solution.py:38
  5.8 6.6 %collective-permute-start.1 = (f32[8,2048]{1,0:T(8,128)}, f32[8,2048]{1,0:T(8,128)S(1)}, u32[]{:S(2)}, u32[]{:S(2)}) collective-permute-start(f32[8,2048]{1,0:T(8,128)} %refs_4_.3), channel_id=1, source_target_pairs={{0,4},{1,5},{2,6},{3,7},{4,0},{5,1},{6,2},{7,3},{8,12},{9,13},{10,... | collective-permute-start | bytes 196616 | tf_op jit(solution)/shard_map/ppermute | solution.py:38
  5.8 6.6 %collective-permute-start.2 = (f32[8,2048]{1,0:T(8,128)}, f32[8,2048]{1,0:T(8,128)S(1)}, u32[]{:S(2)}, u32[]{:S(2)}) collective-permute-start(f32[8,2048]{1,0:T(8,128)} %refs_4_.3), channel_id=1, source_target_pairs={{0,2},{1,3},{2,0},{3,1},{4,6},{5,7},{6,4},{7,5},{8,10},{9,11},{10,... | collective-permute-start | bytes 196616 | tf_op jit(solution)/shard_map/ppermute | solution.py:38
  12.4 1.6 %collective-permute-start.3 = (f32[32,2048]{1,0:T(8,128)S(1)}, f32[32,2048]{1,0:T(8,128)S(1)}, u32[]{:S(2)}, u32[]{:S(2)}) collective-permute-start(f32[32,2048]{1,0:T(8,128)S(1)} %lay_rows.1.own_ref), channel_id=1, source_target_pairs={{0,1},{1,0},{2,3},{3,2},{4,5},{5,4},{6,7},{7,6},{8,9},{9,8},{10,11... | collective-permute-start | bytes 786440 | tf_op jit(solution)/shard_map/ppermute | solution.py:38
  18.0 11.4 %copy-start = (f32[16,4096]{1,0:T(8,128)S(1)}, f32[16,4096]{1,0:T(8,128)}, u32[]{:S(2)}) copy-start(f32[16,4096]{1,0:T(8,128)} %refs_4_.5) | copy-start | bytes 786436
  18.0 11.0 %collective-permute-start.10 = (f32[16,2048]{1,0:T(8,128)S(1)}, f32[16,2048]{1,0:T(8,128)S(1)}, u32[]{:S(2)}, u32[]{:S(2)}) collective-permute-start(f32[16,2048]{1,0:T(8,128)S(1)} %get-tuple-element.28), channel_id=1, source_target_pairs={{0,8},{8,0},{16,24},{24,16},{1,9},{9,1},{17,25},{25,17},{2,10},{10... | collective-permute-start | bytes 393224 | tf_op jit(solution)/shard_map/ppermute | solution.py:38
  19.7 9.7 %collective-permute-start.11 = (f32[16,2048]{1,0:T(8,128)S(1)}, f32[16,2048]{1,0:T(8,128)S(1)}, u32[]{:S(2)}, u32[]{:S(2)}) collective-permute-start(f32[16,2048]{1,0:T(8,128)S(1)} %get-tuple-element.29), channel_id=1, source_target_pairs={{0,16},{8,24},{16,0},{24,8},{1,17},{9,25},{17,1},{25,9},{2,18},{10... | collective-permute-start | bytes 393224 | tf_op jit(solution)/shard_map/ppermute | solution.py:38
  21.2 8.2 %collective-permute-start.12 = (f32[16,2048]{1,0:T(8,128)S(1)}, f32[16,2048]{1,0:T(8,128)S(1)}, u32[]{:S(2)}, u32[]{:S(2)}) collective-permute-start(f32[16,2048]{1,0:T(8,128)S(1)} %get-tuple-element.30), channel_id=1, source_target_pairs={{0,24},{8,16},{16,8},{24,0},{1,25},{9,17},{17,9},{25,1},{2,26},{10... | collective-permute-start | bytes 393224 | tf_op jit(solution)/shard_map/ppermute | solution.py:38
  25.8 6.9 %collective-permute-start.4 = (f32[16,2048]{1,0:T(8,128)S(1)}, f32[16,2048]{1,0:T(8,128)S(1)}, u32[]{:S(2)}, u32[]{:S(2)}) collective-permute-start(f32[16,2048]{1,0:T(8,128)S(1)} %get-tuple-element.24), channel_id=1, source_target_pairs={{0,8},{8,0},{16,24},{24,16},{1,9},{9,1},{17,25},{25,17},{2,10},{10... | collective-permute-start | bytes 393224 | tf_op jit(solution)/shard_map/ppermute | solution.py:38
  27.5 9.0 %collective-permute-start.5 = (f32[16,2048]{1,0:T(8,128)S(1)}, f32[16,2048]{1,0:T(8,128)S(1)}, u32[]{:S(2)}, u32[]{:S(2)}) collective-permute-start(f32[16,2048]{1,0:T(8,128)S(1)} %get-tuple-element.25), channel_id=1, source_target_pairs={{0,16},{8,24},{16,0},{24,8},{1,17},{9,25},{17,1},{25,9},{2,18},{10... | collective-permute-start | bytes 393224 | tf_op jit(solution)/shard_map/ppermute | solution.py:38
  29.0 7.5 %collective-permute-start.6 = (f32[16,2048]{1,0:T(8,128)S(1)}, f32[16,2048]{1,0:T(8,128)S(1)}, u32[]{:S(2)}, u32[]{:S(2)}) collective-permute-start(f32[16,2048]{1,0:T(8,128)S(1)} %get-tuple-element.26), channel_id=1, source_target_pairs={{0,24},{8,16},{16,8},{24,0},{1,25},{9,17},{17,9},{25,1},{2,26},{10... | collective-permute-start | bytes 393224 | tf_op jit(solution)/shard_map/ppermute | solution.py:38
  29.4 9.8 %collective-permute-start.13 = (f32[16,2048]{1,0:T(8,128)S(1)}, f32[16,2048]{1,0:T(8,128)S(1)}, u32[]{:S(2)}, u32[]{:S(2)}) collective-permute-start(f32[16,2048]{1,0:T(8,128)S(1)} %grad_mine.3.refs_1_.refs_0_), channel_id=1, source_target_pairs={{0,8},{8,0},{16,24},{24,16},{1,9},{9,1},{17,25},{25,17},{2,10},{10... | collective-permute-start | bytes 393224 | tf_op jit(solution)/shard_map/ppermute | solution.py:38
  31.1 10.5 %collective-permute-start.14 = (f32[16,2048]{1,0:T(8,128)S(1)}, f32[16,2048]{1,0:T(8,128)S(1)}, u32[]{:S(2)}, u32[]{:S(2)}) collective-permute-start(f32[16,2048]{1,0:T(8,128)S(1)} %grad_mine.3.refs_1_.refs_0_), channel_id=1, source_target_pairs={{0,16},{8,24},{16,0},{24,8},{1,17},{9,25},{17,1},{25,9},{2,18},{10... | collective-permute-start | bytes 393224 | tf_op jit(solution)/shard_map/ppermute | solution.py:38
  32.7 9.4 %collective-permute-start.15 = (f32[16,2048]{1,0:T(8,128)S(1)}, f32[16,2048]{1,0:T(8,128)S(1)}, u32[]{:S(2)}, u32[]{:S(2)}) collective-permute-start(f32[16,2048]{1,0:T(8,128)S(1)} %grad_mine.3.refs_1_.refs_0_), channel_id=1, source_target_pairs={{0,24},{8,16},{16,8},{24,0},{1,25},{9,17},{17,9},{25,1},{2,26},{10... | collective-permute-start | bytes 393224 | tf_op jit(solution)/shard_map/ppermute | solution.py:38
  36.6 10.9 %collective-permute-start.7 = (f32[16,2048]{1,0:T(8,128)S(1)}, f32[16,2048]{1,0:T(8,128)S(1)}, u32[]{:S(2)}, u32[]{:S(2)}) collective-permute-start(f32[16,2048]{1,0:T(8,128)S(1)} %grad_mine.2.refs_2_.refs_4_), channel_id=1, source_target_pairs={{0,8},{8,0},{16,24},{24,16},{1,9},{9,1},{17,25},{25,17},{2,10},{10... | collective-permute-start | bytes 393224 | tf_op jit(solution)/shard_map/ppermute | solution.py:38
  37.9 9.6 %collective-permute-start.8 = (f32[16,2048]{1,0:T(8,128)S(1)}, f32[16,2048]{1,0:T(8,128)S(1)}, u32[]{:S(2)}, u32[]{:S(2)}) collective-permute-start(f32[16,2048]{1,0:T(8,128)S(1)} %grad_mine.2.refs_2_.refs_4_), channel_id=1, source_target_pairs={{0,16},{8,24},{16,0},{24,8},{1,17},{9,25},{17,1},{25,9},{2,18},{10... | collective-permute-start | bytes 393224 | tf_op jit(solution)/shard_map/ppermute | solution.py:38
  39.2 8.3 %collective-permute-start.9 = (f32[16,2048]{1,0:T(8,128)S(1)}, f32[16,2048]{1,0:T(8,128)S(1)}, u32[]{:S(2)}, u32[]{:S(2)}) collective-permute-start(f32[16,2048]{1,0:T(8,128)S(1)} %grad_mine.2.refs_2_.refs_4_), channel_id=1, source_target_pairs={{0,24},{8,16},{16,8},{24,0},{1,25},{9,17},{17,9},{25,1},{2,26},{10... | collective-permute-start | bytes 393224 | tf_op jit(solution)/shard_map/ppermute | solution.py:38
  52.5 2.9 %collective-permute-start.16 = (f32[4,8,2048]{2,1,0:T(8,128)S(1)}, f32[4,8,2048]{2,1,0:T(8,128)S(1)}, u32[]{:S(2)}, u32[]{:S(2)}) collective-permute-start(f32[4,8,2048]{2,1,0:T(8,128)S(1)} %get-tuple-element.32), channel_id=1, source_target_pairs={{0,1},{1,0},{2,3},{3,2},{4,5},{5,4},{6,7},{7,6},{8,9},{9,8},{10,11... | collective-permute-start | bytes 786440 | tf_op jit(solution)/shard_map/ppermute | solution.py:38
  55.5 15.2 %collective-permute-start.17 = (f32[8,2048]{1,0:T(8,128)S(1)}, f32[8,2048]{1,0:T(8,128)S(1)}, u32[]{:S(2)}, u32[]{:S(2)}) collective-permute-start(f32[8,2048]{1,0:T(8,128)S(1)} %get-tuple-element.34), channel_id=1, source_target_pairs={{0,6},{1,7},{2,4},{3,5},{4,2},{5,3},{6,0},{7,1},{8,14},{9,15},{10,... | collective-permute-start | bytes 196616 | tf_op jit(solution)/shard_map/ppermute | solution.py:38
  59.2 11.5 %collective-permute-start.18 = (f32[8,2048]{1,0:T(8,128)S(1)}, f32[8,2048]{1,0:T(8,128)S(1)}, u32[]{:S(2)}, u32[]{:S(2)}) collective-permute-start(f32[8,2048]{1,0:T(8,128)S(1)} %get-tuple-element.35), channel_id=1, source_target_pairs={{0,4},{1,5},{2,6},{3,7},{4,0},{5,1},{6,2},{7,3},{8,12},{9,13},{10,... | collective-permute-start | bytes 196616 | tf_op jit(solution)/shard_map/ppermute | solution.py:38
  59.2 11.5 %collective-permute-start.19 = (f32[8,2048]{1,0:T(8,128)S(1)}, f32[8,2048]{1,0:T(8,128)S(1)}, u32[]{:S(2)}, u32[]{:S(2)}) collective-permute-start(f32[8,2048]{1,0:T(8,128)S(1)} %get-tuple-element.36), channel_id=1, source_target_pairs={{0,2},{1,3},{2,0},{3,1},{4,6},{5,7},{6,4},{7,5},{8,10},{9,11},{10,... | collective-permute-start | bytes 196616 | tf_op jit(solution)/shard_map/ppermute | solution.py:38
